TPU v7x, 128 devices: a whole 4x4x4 slice. The times are simulated.
128 devices in a mesh: zero: 8 (over y_hi, x), dp: 16 (over z, y_lo, core).
Axes of the slice: x: 4, y: 4 (y_hi: 2, y_lo: 2; y = y_hi * 2 + y_lo), z: 4, core: 2. Of those that a mesh axis runs over, the one named last changes fastest.
Arguments:
- hidden: bfloat16 [16, 1024, 8192], P('dp', 'zero'), may hold values from -6 to 6
- queries: bfloat16 [16, 1024, 4096], P('dp', 'zero'), may hold values from -400 to 400
- grad_out: bfloat16 [16, 1024, 4096], P('dp', 'zero'), may hold values from -6 to 6
- key_weight: bfloat16 [8192, 512], P(('zero', 'dp')), may hold values from -0.0625 to 0.0625
- value_weight: bfloat16 [8192, 512], P(('zero', 'dp')), may hold values from -0.0625 to 0.0625
- doc_lengths: int32 [16, 3], P('dp'), may hold values from 1 to 896, 1024 in all within a row
Outputs:
- d_queries: bfloat16 [16, 1024, 4096], P('dp', 'zero')
- d_hidden: bfloat16 [16, 1024, 8192], P('dp', 'zero')
- grad_key_weight: float32 [8192, 512], P(('zero', 'dp'))
- grad_value_weight: float32 [8192, 512], P(('zero', 'dp'))
Inputs may be any that keep to these rules, and one draw needn't show every extreme that they name: `doc_lengths`: each row holds the lengths of 3 documents packed in order into one group of 1024 tokens, summing to 1024.
All inputs are finite; a program needn't handle non-finite values.
Results may differ from a plain program's by a relative error of at most 0.029.
The roundings to bfloat16 on the way count: a program that leaves them out, or rounds other values in their place, can miss the bound.
Values may be sent and summed in bfloat16 or wider, within the bound.
A program may use at most 128 MiB of HBM per device.

v0:
```python
import jax
import jax.numpy as jnp
from jax import lax
from jax.sharding import PartitionSpec as P

KV_HEADS = 4
HD = 128


ROPE_BASE = 500000.0
NEGATIVE = -1e30


def doc_layout(lengths, group_len):
    doc_ends = jnp.cumsum(lengths)
    places = jnp.arange(group_len, dtype=jnp.int32)
    passed = (doc_ends[None, :] <= places[:, None]).astype(jnp.int32)
    doc_ids = jnp.sum(passed, axis=1)
    before = jnp.sum(passed * lengths[None, :], axis=1)
    return (doc_ids, places - before)


def rope_tables(doc_pos, head_dim):
    half_dim = head_dim // 2
    inverse_freq = ROPE_BASE ** (-2.0 * jnp.arange(half_dim, dtype=jnp.float32) / head_dim)
    angles = doc_pos.astype(jnp.float32)[:, None] * inverse_freq[None, :]
    angles = jnp.concatenate([angles, angles], axis=1)
    return (jnp.cos(angles), jnp.sin(angles))


def rotate(key_rows, cosine, sine_table, kv_heads):
    row_count = key_rows.shape[0]
    per_head = key_rows.reshape(row_count, kv_heads, -1)
    half_dim = per_head.shape[2] // 2
    turned = jnp.concatenate([-per_head[..., half_dim:], per_head[..., :half_dim]], axis=2)
    result = per_head * cosine[:, None, :] + turned * sine_table[:, None, :]
    return result.reshape(row_count, -1)


def unrotate(grad_rows, cosine, sine_table, kv_heads):
    row_count = grad_rows.shape[0]
    per_head = grad_rows.reshape(row_count, kv_heads, -1)
    half_dim = per_head.shape[2] // 2
    scaled = per_head * sine_table[:, None, :]
    moved_back = jnp.concatenate([scaled[..., half_dim:], -scaled[..., :half_dim]], axis=2)
    return (per_head * cosine[:, None, :] + moved_back).reshape(row_count, -1)


def attend(queries, grad_out, key_rows, value_rows, query_doc, query_at, key_doc, blocks):
    row_count = queries.shape[0]
    key_count, kv_width = key_rows.shape
    kv_heads = KV_HEADS
    head_dim = kv_width // kv_heads
    groups = queries.shape[1] // kv_width
    block_len = key_count // blocks
    score_scale = head_dim ** (-0.5)
    query_heads = queries.reshape(row_count, kv_heads, groups, head_dim)
    grad_heads = grad_out.reshape(row_count, kv_heads, groups, head_dim)

    def block_at(number):
        offset = number * block_len
        key_block = key_rows.reshape(block_len, kv_heads, head_dim)
        value_block = value_rows.reshape(block_len, kv_heads, head_dim)
        key_at = offset + jnp.arange(block_len, dtype=jnp.int32)
        allowed = (query_doc[:, None] == key_doc[None, :]) & (query_at[:, None] >= key_at[None, :])
        return (key_block, value_block, allowed, offset)

    def scores(key_block):
        return (
            jnp.einsum("tkgd,skd->kgts", query_heads, key_block, preferred_element_type=jnp.float32)
            * score_scale
        )

    def visit_block(number, state_in, work):
        key_block, value_block, allowed, offset = block_at(number)
        return work(state_in, key_block, value_block, allowed, offset)

    def sweep(work, initial):

        def stepper(number, state_in):
            return visit_block(number, state_in, work)

        return lax.fori_loop(0, blocks, stepper, initial)

    state_shape = (kv_heads, groups, row_count)

    def total_work(state_in, key_block, value_block, allowed, offset):
        running_max, summed = state_in
        block_scores = scores(key_block)
        block_max = jnp.max(jnp.where(allowed, block_scores, NEGATIVE), axis=-1)
        new_max = jnp.maximum(running_max, block_max)
        terms = jnp.where(allowed, jnp.exp(block_scores - new_max[..., None]), 0.0)
        return (new_max, summed * jnp.exp(running_max - new_max) + jnp.sum(terms, axis=-1))

    running_max, summed = sweep(
        total_work,
        (jnp.full(state_shape, NEGATIVE, jnp.float32), jnp.zeros(state_shape, jnp.float32)),
    )
    log_total = running_max + jnp.log(summed)

    def output_work(state_in, key_block, value_block, allowed, offset):
        weights = jnp.where(allowed, jnp.exp(scores(key_block) - log_total[..., None]), 0.0).astype(
            jnp.bfloat16
        )
        return state_in + jnp.einsum(
            "kgts,skd->kgtd", weights, value_block, preferred_element_type=jnp.float32
        )

    attended = sweep(output_work, jnp.zeros(state_shape + (head_dim,), jnp.float32))
    delta = jnp.einsum("tkgd,kgtd->kgt", grad_heads.astype(jnp.float32), attended)

    def back_work(state_in, key_block, value_block, allowed, offset):
        dquery, dkey_all, dvalue_all = state_in
        weights = jnp.where(allowed, jnp.exp(scores(key_block) - log_total[..., None]), 0.0)
        weights_low = weights.astype(jnp.bfloat16)
        dvalue_block = jnp.einsum(
            "kgts,tkgd->skd", weights_low, grad_heads, preferred_element_type=jnp.float32
        )
        dweights = jnp.einsum(
            "tkgd,skd->kgts", grad_heads, value_block, preferred_element_type=jnp.float32
        )
        dscores = (weights * (dweights - delta[..., None])).astype(jnp.bfloat16)
        dquery = (
            dquery
            + jnp.einsum("kgts,skd->tkgd", dscores, key_block, preferred_element_type=jnp.float32)
            * score_scale
        )
        dkey_block = (
            jnp.einsum("kgts,tkgd->skd", dscores, query_heads, preferred_element_type=jnp.float32)
            * score_scale
        )
        dkey_all = dkey_block.reshape(block_len, kv_width)
        dvalue_all = dvalue_block.reshape(block_len, kv_width)
        return (dquery, dkey_all, dvalue_all)

    initial = (
        jnp.zeros((row_count, kv_heads, groups, head_dim), jnp.float32),
        jnp.zeros((key_count, kv_width), jnp.float32),
        jnp.zeros((key_count, kv_width), jnp.float32),
    )
    dquery, dkey_all, dvalue_all = sweep(back_work, initial)
    return (dquery.reshape(row_count, -1), dkey_all, dvalue_all)


def local(hidden, queries, grad_out, key_weight, value_weight, doc_lengths):
    tokens = hidden.shape[1]
    members = lax.axis_size("zero")
    group_len = tokens * members
    rows_in = hidden[0]
    query_in = queries[0]
    grad_in = grad_out[0]
    lengths = doc_lengths[0]
    full_key, full_value = (
        lax.all_gather(key_weight, ("zero", "dp"), axis=0, tiled=True),
        lax.all_gather(value_weight, ("zero", "dp"), axis=0, tiled=True),
    )
    doc_ids, doc_pos = doc_layout(lengths, group_len)
    offset = lax.axis_index("zero") * tokens
    my_pos = lax.dynamic_slice_in_dim(doc_pos, offset, tokens, 0)
    cosine, sine_table = rope_tables(my_pos, HD)
    key_local = rotate(
        jnp.dot(rows_in, full_key, preferred_element_type=jnp.float32), cosine, sine_table, KV_HEADS
    ).astype(jnp.bfloat16)
    value_local = jnp.dot(rows_in, full_value, preferred_element_type=jnp.float32).astype(
        jnp.bfloat16
    )
    key_rows, value_rows = (
        lax.all_gather(key_local, "zero", axis=0, tiled=True),
        lax.all_gather(value_local, "zero", axis=0, tiled=True),
    )
    query_doc = lax.dynamic_slice_in_dim(doc_ids, offset, tokens, 0)
    query_at = offset + jnp.arange(tokens, dtype=jnp.int32)
    dquery, dkey_part, dvalue_part = attend(
        query_in, grad_in, key_rows, value_rows, query_doc, query_at, doc_ids, 1
    )
    dkeys, dvalues = (
        lax.psum_scatter(
            dkey_part.astype(jnp.bfloat16), "zero", scatter_dimension=0, tiled=True
        ).astype(jnp.float32),
        lax.psum_scatter(
            dvalue_part.astype(jnp.bfloat16), "zero", scatter_dimension=0, tiled=True
        ).astype(jnp.float32),
    )
    dkeys_pre = unrotate(dkeys, cosine, sine_table, KV_HEADS).astype(jnp.bfloat16)
    dvalues_low = dvalues.astype(jnp.bfloat16)
    dhidden = jnp.dot(dkeys_pre, full_key.T, preferred_element_type=jnp.float32) + jnp.dot(
        dvalues_low, full_value.T, preferred_element_type=jnp.float32
    )
    key_terms = jnp.dot(rows_in.T, dkeys_pre, preferred_element_type=jnp.float32)
    value_terms = jnp.dot(rows_in.T, dvalues_low, preferred_element_type=jnp.float32)
    key_group, value_group = (
        lax.psum_scatter(
            key_terms.astype(jnp.bfloat16), "zero", scatter_dimension=0, tiled=True
        ).astype(jnp.float32),
        lax.psum_scatter(
            value_terms.astype(jnp.bfloat16), "zero", scatter_dimension=0, tiled=True
        ).astype(jnp.float32),
    )
    grad_key, grad_value = (
        lax.psum_scatter(key_group, "dp", scatter_dimension=0, tiled=True),
        lax.psum_scatter(value_group, "dp", scatter_dimension=0, tiled=True),
    )
    return (
        dquery.astype(jnp.bfloat16)[None],
        dhidden.astype(jnp.bfloat16)[None],
        grad_key,
        grad_value,
    )


def solution(mesh):
    return jax.shard_map(
        local,
        mesh=mesh,
        in_specs=(
            P("dp", "zero", None),
            P("dp", "zero", None),
            P("dp", "zero", None),
            P(("zero", "dp"), None),
            P(("zero", "dp"), None),
            P("dp", None),
        ),
        out_specs=(
            P("dp", "zero", None),
            P("dp", "zero", None),
            P(("zero", "dp"), None),
            P(("zero", "dp"), None),
        ),
        check_vma=False,
    )
```

profile of v0, /device:TPU:6, one launch (start us, length us, event | category | flops | bytes accessed | tf_op | source)
XLA Modules:
  0.0 1071.8 jit_solution(1999255556880299253)
XLA Ops:
  10.7 203.5 %all-gather.5.cloned.1.call-done = bf16[8192,512]{1,0:T(8,128)(2,1)} async-done(((bf16[64,512]{1,0:T(8,128)(2,1)}), bf16[8192,512]{1,0:T(8,128)(2,1)}) %all-gather.5.cloned.1.call-update) | async-done | bytes 8388624 | tf_op jit(solution)/shard_map/all_gather | solution.py:154
  214.2 11.3 %copy.51 = bf16[512,8192]{1,0:T(8,128)(2,1)} copy(bf16[512,8192]{0,1:T(8,128)(2,1)} %bitcast.116) | data formatting | bytes 16777216 | tf_op jit(solution)/shard_map/dot_general | solution.py:162
  225.6 5.8 fusion.14
  235.1 1.7 copy.62
  237.1 180.7 %all-gather.9.cloned.1.call-done = bf16[8192,512]{1,0:T(8,128)(2,1)} async-done(((bf16[64,512]{1,0:T(8,128)(2,1)}), bf16[8192,512]{1,0:T(8,128)(2,1)}) %all-gather.9.cloned.1.call-update) | async-done | bytes 8388624 | tf_op jit(solution)/shard_map/all_gather | solution.py:155
  417.8 5.3 fusion.20
  423.1 44.8 %all-gather.7.cloned.1.call-done = bf16[1024,512]{0,1:T(8,128)(2,1)} async-done(((bf16[128,512]{0,1:T(8,128)(2,1)}), bf16[1024,512]{0,1:T(8,128)(2,1)}) %all-gather.7.cloned.1.call-update) | async-done | bytes 1048592 | tf_op jit(solution)/shard_map/all_gather | solution.py:168
  467.9 9.8 fusion.2
  477.8 9.4 fusion.5
  487.2 29.7 %all-gather.11.cloned.1.call-done = bf16[1024,512]{1,0:T(8,128)(2,1)} async-done(((bf16[128,512]{1,0:T(8,128)(2,1)}), bf16[1024,512]{1,0:T(8,128)(2,1)}) %all-gather.11.cloned.1.call-update) | async-done | bytes 1048592 | tf_op jit(solution)/shard_map/all_gather | solution.py:169
  516.9 2.2 reshape.153
  519.1 11.9 %fusion.23 = f32[4,8,128,128]{3,2,1,0:T(8,128)} fusion(bf16[1024,4,128,1]{2,1,0,3:T(4,128)(2,1)} %bitcast.127, f32[4,1024,128,8]{2,1,3,0:T(8,128)} %get-tuple-element.112, f32[4,8,128]{2,1,0:T(8,128)S(1)} %log_add_fusion, pred[128,1024]{0,1:T(8,128)(4,1)S(1)} %fusion.26), kind=kOutput, calls=%fused_computation.32 | convolution fusion | flops 1090519040 | bytes 20070400 | tf_op jit(solution)/shard_map/while/body/eval_jaxpr/kgts,skd->kgtd/dot_general | solution.py:105
  531.0 3.0 multiply_reduce_fusion
  534.0 9.1 fusion.1
  543.1 3.2 copy-done.1
  546.3 3.8 fusion.13
  550.1 2.3 copy.88
  552.5 8.9 bitcast_convert_fusion
  561.4 2.3 copy.90
  563.8 59.6 %reduce-scatter.19.cloned.1.call-done = bf16[128,512]{1,0:T(8,128)(2,1)} async-done(((bf16[1024,512]{1,0:T(8,128)(2,1)}), bf16[128,512]{1,0:T(8,128)(2,1)}) %reduce-scatter.19.cloned.1.call-update) | async-done | bytes 131088
  624.6 5.6 fusion.9
  630.2 68.2 %reduce-scatter.21.cloned.1.call-done = bf16[128,512]{1,0:T(8,128)(2,1)} async-done(((bf16[1024,512]{1,0:T(8,128)(2,1)}), bf16[128,512]{1,0:T(8,128)(2,1)}) %reduce-scatter.21.cloned.1.call-update) | async-done | bytes 131088
  698.4 6.5 fusion.10
  705.0 109.8 %reduce-scatter.15.cloned.1.call-done = bf16[1024,512]{0,1:T(8,128)(2,1)} async-done(((bf16[8192,512]{0,1:T(8,128)(2,1)}), bf16[1024,512]{0,1:T(8,128)(2,1)}) %reduce-scatter.15.cloned.1.call-update) | async-done | bytes 1048592 | tf_op jit(solution)/shard_map/reduce_scatter | solution.py:192
  814.8 2.6 copy.92
  817.4 113.9 %reduce-scatter.17.cloned.1.call-done = bf16[1024,512]{0,1:T(8,128)(2,1)} async-done(((bf16[8192,512]{0,1:T(8,128)(2,1)}), bf16[1024,512]{0,1:T(8,128)(2,1)}) %reduce-scatter.17.cloned.1.call-update) | async-done | bytes 1048592 | tf_op jit(solution)/shard_map/reduce_scatter | solution.py:195
  931.4 2.6 copy.94
  934.0 5.0 multiply_convert_fusion
  940.3 6.3 fusion.39
  946.7 7.6 fusion.12
  954.3 44.6 %reduce-scatter.23.cloned.1.call-done = f32[64,512]{1,0:T(8,128)} async-done(((f32[1024,512]{1,0:T(8,128)}), f32[64,512]{1,0:T(8,128)}) %reduce-scatter.23.cloned.1.call-update) | async-done | bytes 131088
  998.9 66.0 %reduce-scatter.25.cloned.1.call-done = f32[64,512]{1,0:T(8,128)} async-done(((f32[1024,512]{1,0:T(8,128)}), f32[64,512]{1,0:T(8,128)}) %reduce-scatter.25.cloned.1.call-update) | async-done | bytes 131088
  (62 shorter events, 10.2 us)
Async XLA Ops:
  7.2 218.4 %copy-start = (bf16[1,128,8192]{2,1,0:T(8,128)(2,1)S(1)}, bf16[1,128,8192]{2,1,0:T(8,128)(2,1)}, u32[]{:S(2)}) copy-start(bf16[1,128,8192]{2,1,0:T(8,128)(2,1)} %param.6) | copy-start | bytes 6291460
  7.2 207.0 %all-gather.5.cloned.1.call-start = ((), (), s32[]{:S(2)}) async-start(), calls=%async_computation.6 | async-start | bytes 8454144 | tf_op jit(solution)/shard_map/all_gather | solution.py:154
  7.9 409.8 %all-gather.9.cloned.1.call-start = ((), (), s32[]{:S(2)}) async-start(), calls=%async_computation.8 | async-start | bytes 8454144 | tf_op jit(solution)/shard_map/all_gather | solution.py:155
  8.7 459.3 %all-gather.7.cloned.1.call-start = ((), (), s32[]{:S(2)}) async-start(), calls=%async_computation.7 | async-start | bytes 1179648 | tf_op jit(solution)/shard_map/all_gather | solution.py:168
  10.7 220.7 %copy-start.5 = (f32[128,128]{0,1:T(8,128)}, f32[128,128]{0,1:T(8,128)S(1)}, u32[]{:S(2)}) copy-start(f32[128,128]{0,1:T(8,128)S(1)} %get-tuple-element.109) | copy-start | bytes 196612
  10.7 220.7 %copy-start.7 = (f32[128,128]{0,1:T(8,128)}, f32[128,128]{0,1:T(8,128)S(1)}, u32[]{:S(2)}) copy-start(f32[128,128]{0,1:T(8,128)S(1)} %get-tuple-element.110) | copy-start | bytes 196612
  225.6 6.8 copy-start.3
  232.2 284.7 %all-gather.11.cloned.1.call-start = ((), (), s32[]{:S(2)}) async-start(), calls=%async_computation.9 | async-start | bytes 1179648 | tf_op jit(solution)/shard_map/all_gather | solution.py:169
  423.1 200.4 %reduce-scatter.19.cloned.1.call-start = ((), (), s32[]{:S(2)}) async-start(), calls=%async_computation.12 | async-start | bytes 1179648
  534.0 12.3 %copy-start.2 = (bf16[1,128,4096]{1,2,0:T(8,128)(2,1)S(1)}, bf16[1,128,4096]{1,2,0:T(8,128)(2,1)}, u32[]{:S(2)}) copy-start(bf16[1,128,4096]{1,2,0:T(8,128)(2,1)} %copy.96) | copy-start | bytes 3145732
  543.1 3.2 copy-start.1
  546.3 6.2 copy-start.4
  552.4 72.0 %copy-start.8 = (f32[128,128]{0,1:T(8,128)S(1)}, f32[128,128]{0,1:T(8,128)}, u32[]{:S(2)}) copy-start(f32[128,128]{0,1:T(8,128)} %copy-done.7) | copy-start | bytes 196612
  552.4 72.1 %copy-start.6 = (f32[128,128]{0,1:T(8,128)S(1)}, f32[128,128]{0,1:T(8,128)}, u32[]{:S(2)}) copy-start(f32[128,128]{0,1:T(8,128)} %copy-done.5) | copy-start | bytes 196612
  552.4 146.0 %reduce-scatter.21.cloned.1.call-start = ((), (), s32[]{:S(2)}) async-start(), calls=%async_computation.13 | async-start | bytes 1179648
  563.8 251.0 %reduce-scatter.15.cloned.1.call-start = ((), (), s32[]{:S(2)}) async-start(), calls=%async_computation.10 | async-start | bytes 9437184 | tf_op jit(solution)/shard_map/reduce_scatter | solution.py:192
  630.2 301.2 %reduce-scatter.17.cloned.1.call-start = ((), (), s32[]{:S(2)}) async-start(), calls=%async_computation.11 | async-start | bytes 9437184 | tf_op jit(solution)/shard_map/reduce_scatter | solution.py:195
  704.9 293.9 %reduce-scatter.23.cloned.1.call-start = ((), (), s32[]{:S(2)}) async-start(), calls=%async_computation.14 | async-start | bytes 2228224
  817.4 247.5 %reduce-scatter.25.cloned.1.call-start = ((), (), s32[]{:S(2)}) async-start(), calls=%async_computation.15 | async-start | bytes 2228224
  939.0 7.6 copy-start.9
Sparse Core Ops, SparseCore 0:
  9.7 204.4 all-gather.4
  215.9 201.7 all-gather.8
  420.5 47.3 all-gather.6
  470.7 46.1 all-gather.10
  552.5 70.8 reduce-scatter.18
  627.4 70.9 reduce-scatter.20
  702.3 112.4 reduce-scatter.14
  818.7 112.6 reduce-scatter.16
  934.4 64.4 reduce-scatter.22
  1001.7 63.1 reduce-scatter.24
where the time goes:
time: 1070 us
  waiting for transfers between devices  922 us (86%)
  matrix products  85.6 us (8%)
  local copies, waits for them, and re-layouts  33.5 us (3%)
  other arithmetic  15.4 us (1%)
  between operations  14.4 us (1%)
    unnamed x14, waiting for transfers between devices  240 us
    all_gather x1, waiting for transfers between devices, local(): lax.all_gather(key_weight, ('zero', 'dp'), axis=0, tiled=True)  203 us
    all_gather x1, waiting for transfers between devices, local(): lax.all_gather(value_weight, ('zero', 'dp'), axis=0, tiled=True)  181 us
    reduce_scatter x1, waiting for transfers between devices, local(): lax.psum_scatter(value_terms.astype(jnp.bfloat16), 'zero', scatter_dimens...  114 us
    reduce_scatter x1, waiting for transfers between devices, local(): lax.psum_scatter(key_terms.astype(jnp.bfloat16), 'zero', scatter_dimensio...  110 us
    all_gather x1, waiting for transfers between devices, local(): lax.all_gather(key_local, 'zero', axis=0, tiled=True)  44.8 us
    all_gather x1, waiting for transfers between devices, local(): lax.all_gather(value_local, 'zero', axis=0, tiled=True)  29.7 us
  transfers between devices with their start and end apart: 10, of which 10 were waited for; matrix products, arithmetic and copies ran while one was open for 9% of the time, Pallas kernels for 0%

commit v1 on v0

v1 whole, which is shorter than its diff:
```python
import functools

import jax
import jax.numpy as jnp
from jax import lax
from jax.experimental import pallas as pl
from jax.experimental.pallas import tpu as pltpu
from jax.sharding import PartitionSpec as P

KV_HEADS = 4
HD = 128
ROPE_BASE = 500000.0
NEGATIVE = -1e30
LOG2E = 1.4426950408889634
MESH = pl.DeviceIdType.MESH
TOK = 128
WIDE = 8192
ANY = pl.BlockSpec(memory_space=pl.ANY)
VMEM = pl.BlockSpec(memory_space=pltpu.VMEM)
BF = jnp.bfloat16
F32 = jnp.float32


def doc_layout(lengths, group_len):
    doc_ends = jnp.cumsum(lengths)
    places = jnp.arange(group_len, dtype=jnp.int32)
    passed = (doc_ends[None, :] <= places[:, None]).astype(jnp.int32)
    doc_ids = jnp.sum(passed, axis=1)
    before = jnp.sum(passed * lengths[None, :], axis=1)
    return (doc_ids, places - before)


def rope_tables(doc_pos, head_dim):
    half_dim = head_dim // 2
    inverse_freq = ROPE_BASE ** (-2.0 * jnp.arange(half_dim, dtype=jnp.float32) / head_dim)
    angles = doc_pos.astype(jnp.float32)[:, None] * inverse_freq[None, :]
    angles = jnp.concatenate([angles, angles], axis=1)
    return (jnp.cos(angles), jnp.sin(angles))


def rotate(key_rows, cosine, sine_table, kv_heads):
    row_count = key_rows.shape[0]
    per_head = key_rows.reshape(row_count, kv_heads, -1)
    half_dim = per_head.shape[2] // 2
    turned = jnp.concatenate([-per_head[..., half_dim:], per_head[..., :half_dim]], axis=2)
    return per_head * cosine[:, None, :] + turned * sine_table[:, None, :]


def place():
    j, i = lax.axis_index("zero"), lax.axis_index("dp")
    return j // 4, j % 4, i // 4, (i // 2) % 2, i % 2


def device(u, x, z, w, c):
    return (u * 4 + x, z * 4 + w * 2 + c)


class Peers:
    def __init__(self):
        self.u, self.x, self.z, self.w, self.c = place()

    def along_x(self, d):
        return device(self.u, (self.x + d) % 4, self.z, self.w, self.c)

    def along_z(self, d):
        return device(self.u, self.x, (self.z + d) % 4, self.w, self.c)

    def y_at(self, d):
        y = (2 * self.u + self.w + d) % 4
        return y // 2, y % 2

    def along_y(self, d):
        u, w = self.y_at(d)
        return device(u, self.x, self.z, w, self.c)

    def in_group(self, du, dx):
        return device((self.u + du) % 2, (self.x + dx) % 4, self.z, self.w, self.c)

    def on_plane(self, dy, dx):
        u, w = self.y_at(dy)
        return device(u, (self.x + dx) % 4, self.z, w, self.c)

    def sibling(self):
        return device(self.u, self.x, self.z, self.w, 1 - self.c)


def meet(devices):
    barrier = pltpu.get_barrier_semaphore()
    for one in devices:
        pl.semaphore_signal(barrier, inc=1, device_id=one, device_id_type=MESH)
    pl.semaphore_wait(barrier, len(devices))


class Copies:
    def __init__(self, send, recv):
        self.send, self.recv, self.used = send, recv, 0

    def make(self, src, dst, to):
        at = self.used
        self.used += 1
        return pltpu.make_async_remote_copy(
            src_ref=src,
            dst_ref=dst,
            send_sem=self.send.at[at],
            recv_sem=self.recv.at[at],
            device_id=to,
            device_id_type=MESH,
        )

    def start(self, src, dst, to):
        copy = self.make(src, dst, to)
        copy.start()
        return copy


GROUP = [(du, dx) for du in (1, 0) for dx in (2, 1, 3, 0)][:-1]
PLANE = [(dy, dx) for dy in (2, 1, 3, 0) for dx in (2, 1, 3, 0)][:-1]
STEPS = (2, 1, 3)


def comm_call(kernel, number, outs, in_specs, out_specs, remote, local, scratch=()):
    return pl.pallas_call(
        kernel,
        out_shape=outs,
        in_specs=in_specs,
        out_specs=out_specs,
        scratch_shapes=[
            pltpu.SemaphoreType.DMA((remote,)),
            pltpu.SemaphoreType.DMA((remote,)),
            pltpu.SemaphoreType.DMA((local,)),
            *scratch,
        ],
        compiler_params=pltpu.CompilerParams(
            collective_id=number, has_side_effects=True, vmem_limit_bytes=48 << 20
        ),
    )


def spread_kernel(hidden, query, wkey, wvalue, hid_g, wk, wv, q_h, send, recv, here):
    p = Peers()
    u, x, z, w, c = p.u, p.x, p.z, p.w, p.c
    cp = Copies(send, recv)
    local = [
        pltpu.make_async_copy(wkey, wk.at[u, x, w, c], here.at[0]),
        pltpu.make_async_copy(wvalue, wv.at[u, x, w, c], here.at[1]),
        pltpu.make_async_copy(
            query.at[:, pl.ds(pl.multiple_of(x * 1024, 1024), 1024)], q_h.at[x], here.at[2]
        ),
    ]
    for one in local:
        one.start()
    own_pieces = []
    for piece in range(8):
        start = pl.multiple_of((piece * 4 + z) * 256, 256)
        own_pieces.append(
            pltpu.make_async_copy(
                hidden.at[:, pl.ds(start, 256)],
                hid_g.at[z, :, pl.ds(piece * 256, 256)],
                here.at[3 + piece],
            )
        )
        own_pieces[-1].start()
    meet(
        [p.along_x(d) for d in STEPS]
        + [p.along_y(d) for d in STEPS]
        + [p.along_z(d) for d in STEPS]
        + [p.sibling()]
    )
    key_y = [cp.start(wkey, wk.at[u, x, w, c], p.along_y(d)) for d in STEPS]
    value_x = [cp.start(wvalue, wv.at[u, x, w, c], p.along_x(d)) for d in STEPS]
    whole = []
    for d in STEPS:
        there = (z + d) % 4
        at = cp.used
        for piece in range(8):
            start = pl.multiple_of((piece * 4 + there) * 256, 256)
            cp.used = at
            cp.start(
                hidden.at[:, pl.ds(start, 256)],
                hid_g.at[z, :, pl.ds(piece * 256, 256)],
                p.along_z(d),
            )
        cp.used = at
        came = (z + 4 - d) % 4
        whole.append(cp.make(hid_g.at[came], hid_g.at[came], p.along_z(d)))
    local[0].wait()
    for one in key_y:
        one.wait_recv()
    column = wk.at[:, x, :, c]
    key_x = [cp.start(column, column, p.along_x(d)) for d in STEPS]
    to_core = [cp.start(column, column, p.sibling())]
    local[1].wait()
    for one in value_x:
        one.wait_recv()
    row = wv.at[u, :, w, c]
    value_y = [cp.start(row, row, p.along_y(d)) for d in STEPS]
    to_core.append(cp.start(row, row, p.sibling()))
    sent_q = []
    for d in STEPS:
        there = (x + d) % 4
        start = pl.multiple_of(there * 1024, 1024)
        sent_q.append(cp.start(query.at[:, pl.ds(start, 1024)], q_h.at[x], p.along_x(d)))
    for d, one in zip((1, 3, 2), (key_x[1], key_x[2], key_x[0])):
        one.wait_recv()
        column = wk.at[:, (x + 4 - d) % 4, :, c]
        to_core.append(cp.start(column, column, p.sibling()))
    for d, one in zip((1, 3, 2), (value_y[1], value_y[2], value_y[0])):
        one.wait_recv()
        from_u, from_w = p.y_at(4 - d)
        row = wv.at[from_u, :, from_w, c]
        to_core.append(cp.start(row, row, p.sibling()))
    for one in to_core + sent_q + whole:
        one.wait_recv()
    for one in key_y + value_x + key_x + value_y + to_core + sent_q + whole:
        one.wait_send()
    for one in local[2:] + own_pieces:
        one.wait()


def spread(hidden, query, wkey, wvalue):
    shape = jax.ShapeDtypeStruct
    return comm_call(
        spread_kernel,
        0,
        (
            shape((4, TOK, 2048), BF),
            shape((2, 4, 2, 2, 64, 512), BF),
            shape((2, 4, 2, 2, 64, 512), BF),
            shape((4, TOK, 1024), BF),
        ),
        [ANY] * 4,
        (ANY,) * 4,
        26,
        11,
    )(hidden, query, wkey, wvalue)


def partials_kernel(kp, vp, grad, k_in, v_in, go_h, send, recv, here):
    p = Peers()
    x, z = p.x, p.z
    cp = Copies(send, recv)
    own = [
        pltpu.make_async_copy(kp.at[z], k_in.at[z], here.at[0]),
        pltpu.make_async_copy(vp.at[z], v_in.at[z], here.at[1]),
        pltpu.make_async_copy(
            grad.at[:, pl.ds(pl.multiple_of(x * 1024, 1024), 1024)], go_h.at[x], here.at[2]
        ),
    ]
    for one in own:
        one.start()
    meet([p.along_x(d) for d in STEPS] + [p.along_z(d) for d in STEPS])
    sent = []
    for d in STEPS:
        there = (z + d) % 4
        sent.append(cp.start(kp.at[there], k_in.at[z], p.along_z(d)))
        sent.append(cp.start(vp.at[there], v_in.at[z], p.along_z(d)))
    for d in STEPS:
        start = pl.multiple_of(((x + d) % 4) * 1024, 1024)
        sent.append(cp.start(grad.at[:, pl.ds(start, 1024)], go_h.at[x], p.along_x(d)))
    for one in sent:
        one.wait()
    for one in own:
        one.wait()


def partials(kp, vp, grad):
    shape = jax.ShapeDtypeStruct
    return comm_call(
        partials_kernel,
        1,
        (shape((4, TOK, 512), F32), shape((4, TOK, 512), BF), shape((4, TOK, 1024), BF)),
        [ANY] * 3,
        (ANY,) * 3,
        9,
        3,
    )(kp, vp, grad)


def heads_kernel(kv, kv_h, send, recv, here):
    p = Peers()
    u, x = p.u, p.x
    cp = Copies(send, recv)

    def head(at):
        return kv.at[:, pl.ds(pl.multiple_of(at * 256, 256), 256)]

    own = pltpu.make_async_copy(head(x), kv_h.at[u, x], here.at[0])
    own.start()
    meet([p.in_group(du, dx) for du, dx in GROUP])
    sent = [
        cp.start(head((x + dx) % 4), kv_h.at[u, x], p.in_group(du, dx)) for du, dx in GROUP
    ]
    for one in sent:
        one.wait()
    own.wait()


def heads(kv):
    shape = jax.ShapeDtypeStruct
    return comm_call(
        heads_kernel, 2, shape((2, 4, TOK, 256), BF), [ANY], ANY, 7, 1
    )(kv)


ROWS = 256


def attend_kernel(u_ref, low_ref, q, go, kv, dq, dkv, bias, kt, dk_sum, dv_sum):
    block, head = pl.program_id(0), pl.program_id(1)
    u = u_ref[0]
    scale = HD**-0.5

    @pl.when((block == 0) & (head == 0))
    def _():
        dk_sum[...] = jnp.zeros_like(dk_sum)
        dv_sum[...] = jnp.zeros_like(dv_sum)
        kt[...] = kv[:, :HD].astype(F32).T.astype(BF)

    @pl.when(head == 0)
    def _():
        key_at = lax.broadcasted_iota(jnp.int32, (1024, ROWS), 0)
        query_at = (u * 2 + block) * ROWS + lax.broadcasted_iota(jnp.int32, (1024, ROWS), 1)
        allowed = (key_at <= query_at) & (key_at >= low_ref[...])
        bias[...] = jnp.where(allowed, 0.0, NEGATIVE)

    def work(keys):
        query, grad = q[...], go[...]
        key, value = kv[:keys, :HD], kv[:keys, HD:]
        contract = (((1,), (1,)), ((), ()))
        s = lax.dot_general(key, query, contract, preferred_element_type=F32) + bias[:keys]
        top = jnp.max(s, axis=0, keepdims=True)
        e = jnp.exp2((s - top) * (scale * LOG2E))
        weights = e * (1.0 / jnp.sum(e, axis=0, keepdims=True))
        low = weights.astype(BF)
        dw = lax.dot_general(value, grad, contract, preferred_element_type=F32)
        delta = jnp.sum(low.astype(F32) * dw, axis=0, keepdims=True)
        ds = (weights * (dw - delta)).astype(BF)
        dv_sum[:keys] += jnp.dot(low, grad, preferred_element_type=F32)
        dk_sum[:keys] += jnp.dot(ds, query, preferred_element_type=F32)
        turned = jnp.dot(kt[:, :keys], ds, preferred_element_type=F32)
        dq[...] = (turned.T * scale).astype(BF)

    for count in range(1, 5):
        pl.when(u * 2 + block == count - 1)(functools.partial(work, count * ROWS))

    @pl.when((block == 1) & (head == 7))
    def _():
        dkv[:, :HD] = (dk_sum[...] * scale).astype(BF)
        dkv[:, HD:] = dv_sum[...].astype(BF)


def attend(u, low, q_h, go_h, kv_h):
    shape = jax.ShapeDtypeStruct
    one_head = pl.BlockSpec((ROWS, HD), lambda i, g, *_: (i, g))
    whole = pl.BlockSpec((1024, 256), lambda i, g, *_: (0, 0))
    return pl.pallas_call(
        attend_kernel,
        grid_spec=pltpu.PrefetchScalarGridSpec(
            num_scalar_prefetch=1,
            grid=(2, 8),
            in_specs=[
                pl.BlockSpec((1, ROWS), lambda i, g, *_: (0, i)),
                one_head,
                one_head,
                whole,
            ],
            out_specs=[one_head, whole],
            scratch_shapes=[
                pltpu.VMEM((1024, ROWS), F32),
                pltpu.VMEM((HD, 1024), BF),
                pltpu.VMEM((1024, HD), F32),
                pltpu.VMEM((1024, HD), F32),
            ],
        ),
        out_shape=[shape((512, 1024), BF), shape((1024, 256), BF)],
        compiler_params=pltpu.CompilerParams(vmem_limit_bytes=48 << 20),
    )(u, low, q_h, go_h, kv_h)


def collect_kernel(dkv, dq_h, cosine, sine, dkv_g, dq, send, recv, here, came, own_rows):
    p = Peers()
    u, x, z = p.u, p.x, p.z
    cp = Copies(send, recv)

    def head(at):
        return dq.at[:, pl.ds(pl.multiple_of(at * 1024, 1024), 1024)]

    own = [
        pltpu.make_async_copy(dkv.at[u, x], came.at[u, x], here.at[0]),
        pltpu.make_async_copy(dq_h.at[x], head(x), here.at[1]),
    ]
    for one in own:
        one.start()
    meet([p.in_group(du, dx) for du, dx in GROUP] + [p.along_z(d) for d in STEPS])
    sent = [
        cp.start(dkv.at[(u + du) % 2, (x + dx) % 4], came.at[u, x], p.in_group(du, dx))
        for du, dx in GROUP
    ]
    sent_q = [cp.start(dq_h.at[(x + d) % 4], head(x), p.along_x(d)) for d in STEPS]
    for one in sent:
        one.wait_recv()
    own[0].wait()
    cos, sin = cosine[...], sine[...]
    for h in range(KV_HEADS):
        total = came[0, h].astype(F32) + came[1, h].astype(F32)
        dk = total[:, :HD]
        scaled = dk * sin
        half = HD // 2
        back = jnp.concatenate([scaled[:, half:], -scaled[:, :half]], axis=1)
        own_rows[:, h * HD : (h + 1) * HD] = (dk * cos + back).astype(BF)
        own_rows[:, 512 + h * HD : 512 + (h + 1) * HD] = total[:, HD:].astype(BF)
    keep = pltpu.make_async_copy(own_rows, dkv_g.at[z], here.at[2])
    keep.start()
    sent_z = [cp.start(own_rows, dkv_g.at[z], p.along_z(d)) for d in STEPS]
    for one in sent_z + sent_q:
        one.wait_recv()
    for one in sent + sent_z + sent_q:
        one.wait_send()
    own[1].wait()
    keep.wait()


def collect(dkv, dq_h, cosine, sine):
    shape = jax.ShapeDtypeStruct
    return comm_call(
        collect_kernel,
        3,
        (shape((4, TOK, 1024), BF), shape((TOK, 4096), BF)),
        [ANY, ANY, VMEM, VMEM],
        (ANY, ANY),
        13,
        3,
        (pltpu.VMEM((2, 4, TOK, 256), BF), pltpu.VMEM((TOK, 1024), BF)),
    )(dkv, dq_h, cosine, sine)


def finish_kernel(dh, gw, dhidden, terms, send, recv, here, mine, other):
    p = Peers()
    u, x, z, w, c = p.u, p.x, p.z, p.w, p.c
    cp = Copies(send, recv)
    order = PLANE + [(0, 0)]
    loads = []
    for k, (dy, dx) in enumerate(order):
        tu, tw = p.y_at(dy)
        loads.append(
            pltpu.make_async_copy(gw.at[tu, (x + dx) % 4, tw, c], mine.at[k], here.at[k])
        )
        loads[-1].start()
    own_pieces = []
    for piece in range(8):
        start = pl.multiple_of((piece * 4 + z) * 256, 256)
        own_pieces.append(
            pltpu.make_async_copy(
                dh.at[z, :, pl.ds(piece * 256, 256)],
                dhidden.at[:, pl.ds(start, 256)],
                here.at[16 + piece],
            )
        )
        own_pieces[-1].start()
    meet(
        [p.on_plane(dy, dx) for dy, dx in PLANE]
        + [p.along_z(d) for d in STEPS]
        + [p.sibling()]
    )
    swapped = []
    for k, (dy, dx) in enumerate(order):
        tu, tw = p.y_at(dy)
        swapped.append(
            cp.start(gw.at[tu, (x + dx) % 4, tw, 1 - c], other.at[k], p.sibling())
        )
    whole = []
    for d in STEPS:
        there = (z + d) % 4
        at = cp.used
        for piece in range(8):
            start = pl.multiple_of((piece * 4 + z) * 256, 256)
            cp.used = at
            cp.start(
                dh.at[there, :, pl.ds(piece * 256, 256)],
                dhidden.at[:, pl.ds(start, 256)],
                p.along_z(d),
            )
        cp.used = at
        whole.append(cp.make(dh.at[there], dh.at[there], p.along_z(d)))
    sent = []
    for k, (dy, dx) in enumerate(order):
        loads[k].wait()
        swapped[k].wait_recv()
        mine[k] = (mine[k].astype(F32) + other[k].astype(F32)).astype(BF)
        if (dy, dx) == (0, 0):
            keep = pltpu.make_async_copy(mine.at[k], terms.at[k], here.at[24])
            keep.start()
        else:
            sent.append(cp.start(mine.at[k], terms.at[k], p.on_plane(dy, dx)))
    for one in sent + whole:
        one.wait_recv()
    for one in sent + whole + swapped:
        one.wait_send()
    for one in own_pieces:
        one.wait()
    keep.wait()


def finish(dh, gw):
    shape = jax.ShapeDtypeStruct
    return comm_call(
        finish_kernel,
        4,
        (shape((TOK, WIDE), BF), shape((16, 64, 1024), BF)),
        [ANY, ANY],
        (ANY, ANY),
        34,
        25,
        (pltpu.VMEM((16, 64, 1024), BF), pltpu.VMEM((16, 64, 1024), BF)),
    )(dh, gw)


def local(hidden, queries, grad_out, key_weight, value_weight, doc_lengths):
    lengths = doc_lengths[0]
    doc_ids, doc_pos = doc_layout(lengths, 1024)
    zero = lax.axis_index("zero")
    half = zero // 4
    my_pos = lax.dynamic_slice_in_dim(doc_pos, zero * TOK, TOK, 0)
    cosine, sine = rope_tables(my_pos, HD)
    first_key = jnp.arange(1024, dtype=jnp.int32) - doc_pos
    low = lax.dynamic_slice_in_dim(first_key, half * 512, 512, 0)[None, :]

    hid_g, wk, wv, q_h = spread(hidden[0], queries[0], key_weight, value_weight)
    hid_g = hid_g.reshape(512, 2048)
    wk, wv = wk.reshape(2048, 512), wv.reshape(2048, 512)
    kp = jnp.dot(hid_g, wk, preferred_element_type=F32).reshape(4, TOK, 512)
    vp = jnp.dot(hid_g, wv, preferred_element_type=F32).astype(BF).reshape(4, TOK, 512)
    k_in, v_in, go_h = partials(kp, vp, grad_out[0])
    k_rows = rotate(jnp.sum(k_in, axis=0), cosine, sine, KV_HEADS)
    v_rows = jnp.sum(v_in.astype(F32), axis=0).reshape(TOK, KV_HEADS, HD)
    kv = jnp.concatenate([k_rows, v_rows], axis=2).astype(BF).reshape(TOK, 1024)
    kv_h = heads(kv).reshape(1024, 256)
    dq_h, dkv = attend(
        half.astype(jnp.int32)[None], low, q_h.reshape(512, 1024), go_h.reshape(512, 1024), kv_h
    )
    dkv_g, dquery = collect(
        dkv.reshape(2, 4, TOK, 256), dq_h.reshape(4, TOK, 1024), cosine, sine
    )
    dkv_g = dkv_g.reshape(512, 1024)
    dh = jnp.dot(dkv_g[:, :512], wk.T, preferred_element_type=F32) + jnp.dot(
        dkv_g[:, 512:], wv.T, preferred_element_type=F32
    )
    gw = jnp.dot(hid_g.T, dkv_g, preferred_element_type=F32).astype(BF)
    dhidden, terms = finish(
        dh.astype(BF).reshape(4, TOK, 2048), gw.reshape(2, 4, 2, 2, 64, 1024)
    )
    grads = jnp.sum(terms.astype(F32), axis=0)
    return dquery[None], dhidden[None], grads[:, :512], grads[:, 512:]


def solution(mesh):
    return jax.shard_map(
        local,
        mesh=mesh,
        in_specs=(
            P("dp", "zero", None),
            P("dp", "zero", None),
            P("dp", "zero", None),
            P(("zero", "dp"), None),
            P(("zero", "dp"), None),
            P("dp", None),
        ),
        out_specs=(
            P("dp", "zero", None),
            P("dp", "zero", None),
            P(("zero", "dp"), None),
            P(("zero", "dp"), None),
        ),
        check_vma=False,
    )
```

time: 1070 us -> 180 us (0.17)
  waiting for transfers between devices: 922 us -> 0 us
  Pallas kernels: 0 us -> 151 us
  matrix products: 85.6 us -> 13.1 us
  local copies, waits for them, and re-layouts: 33.5 us -> 8.26 us
  between operations: 14.4 us -> 0.89 us
  other arithmetic: 15.4 us -> 4.21 us
    all_gather x4 -> x0, waiting for transfers between devices: 459 us -> none  [the longest x1 203 us: local(): lax.all_gather(key_weight, ('zero', 'dp'), axis=0, tiled=True)]
    unnamed x14 -> x0, waiting for transfers between devices: 240 us -> none
    reduce_scatter x2 -> x0, waiting for transfers between devices: 224 us -> none  [the longest x1 114 us: local(): lax.psum_scatter(value_terms.astype(jnp.bfloat16), 'zero', scatter_dimens...]
    pallas_call x0 -> x6, Pallas kernels: none -> 151 us  [the longest x1 38.2 us: finish(): comm_call(finish_kernel, 4, (shape((TOK, WIDE), BF), shape((16, 64, 1024)...]
    dot_general x12 -> x5, matrix products: 85.6 us -> 13.1 us  [the longest x1 4.31 us: local(): gw = jnp.dot(hid_g.T, dkv_g, preferred_element_type=F32).astype(BF)]
    dot_general x2 -> x0, local copies, waits for them, and re-layouts: 11.4 us -> none  [the longest x1 11.3 us: local(): jnp.dot(rows_in, full_key, preferred_element_type=jnp.float32)]
  transfers between devices with their start and end apart: 10 -> 0, of which waited for: 10 -> 0; matrix products, arithmetic and copies ran while one was open for 9% -> 0% of each run, Pallas kernels for 0% -> 0%
where the time goes in v1:
time: 180 us; the launch traced here: 178 us
  Pallas kernels  151 us (84%)
  matrix products  13.1 us (7%)
  local copies, waits for them, and re-layouts  8.26 us (5%)
  other arithmetic  4.21 us (2%)
    pallas_call x1, Pallas kernels, finish(): comm_call(finish_kernel, 4, (shape((TOK, WIDE), BF), shape((16, 64, 1024)...  38.2 us
    pallas_call x1, Pallas kernels, spread(): comm_call(spread_kernel, 0, (shape((4, TOK, 2048), BF), shape((2, 4, 2, 2...  35.3 us
    pallas_call x1, Pallas kernels, collect(): comm_call(collect_kernel, 3, (shape((4, TOK, 1024), BF), shape((TOK, 4096...  30.9 us
    pallas_call x1, Pallas kernels, partials(): comm_call(partials_kernel, 1, (shape((4, TOK, 512), F32), shape((4, TOK,...  21.4 us
    pallas_call x1, Pallas kernels, attend(): pl.pallas_call(attend_kernel, grid_spec=pltpu.PrefetchScalarGridSpec(num_...  13.6 us
    pallas_call x1, Pallas kernels, heads(): comm_call(heads_kernel, 2, shape((2, 4, TOK, 256), BF), [ANY], ANY, 7, 1)  11.9 us
    unnamed x25, local copies, waits for them, and re-layouts  6.69 us
    dot_general x1, matrix products, local(): gw = jnp.dot(hid_g.T, dkv_g, preferred_element_type=F32).astype(BF)  4.31 us

profile of v1, /device:TPU:6, one launch (start us, length us, event | category | flops | bytes accessed | tf_op | source)
XLA Modules:
  0.0 177.7 jit_solution(16728273632116993243)
XLA Ops:
  0.7 0.8 reduce-window.8
  1.5 0.7 select_reduce_fusion
  2.2 0.1 dynamic-slice_convert_fusion
  2.5 0.3 fusion.6
  2.8 1.2 copy-done
  4.0 0.8 copy-done.3
  4.9 0.8 copy-done.4
  5.7 35.3 %shard_map.93 = (bf16[4,128,2048]{2,1,0:T(8,128)(2,1)S(1)}, bf16[2,4,2,2,64,512]{5,4,3,2,1,0:T(8,128)(2,1)}, bf16[2,4,2,2,64,512]{5,4,3,2,1,0:T(8,128)(2,1)}, bf16[4,128,1024]{2,1,0:T(8,128)(2,1)S(1)}) custom-call(bf16[128,8192]{1,0:T(8,128)(2,1)} %bitcast.55, bf16[128,4096]{1,0:T(8,128)(2,1)S(1)} %bitcast.40, bf16[64,512]{1,0:T(8,128)(2,1)S(1)} %copy-done.3, ...), custom_call_target="tpu_custom_call" | custom-call | tf_op jit(solution)/shard_map/pallas_call | solution.py:222
  41.0 3.6 %convolution_convert_fusion = bf16[512,512]{1,0:T(8,128)(2,1)S(1)} fusion(bf16[512,2048]{1,0:T(8,128)(2,1)S(1)} %bitcast.50, bf16[2048,512]{1,0:T(8,128)(2,1)} %bitcast.53), kind=kOutput, calls=%fused_computation.3 | convolution fusion | flops 1074003968 | bytes 4718592 | tf_op jit(solution)/shard_map/dot_general | solution.py:532
  44.7 1.2 fusion.8.kp
  45.9 21.4 %shard_map.94 = (f32[4,128,512]{2,1,0:T(8,128)S(1)}, bf16[4,128,512]{2,1,0:T(8,128)(2,1)S(1)}, bf16[4,128,1024]{2,1,0:T(8,128)(2,1)S(1)}) custom-call(f32[4,128,512]{2,1,0:T(8,128)S(1)} %fusion.8.kp, bf16[4,128,512]{2,1,0:T(8,128)(2,1)S(1)} %bitcast.47, bf16[128,4096]{1,0:T(8,128)(2,1)S(1)} %bitcast.42), custom_call_target="tpu_custom_call" | custom-call | tf_op jit(solution)/shard_map/pallas_call | solution.py:268
  67.4 0.8 copy-done.2
  68.2 1.1 reduce
  69.3 0.7 reshape.146
  70.0 0.1 reduce_sum.37
  70.1 0.1 reshape.145
  70.2 0.2 slice_negate_fusion
  70.4 0.2 fusion.4
  70.6 0.4 copy-done.10
  71.0 0.1 pad_maximum_fusion
  71.2 11.9 %shard_map.95 = bf16[2,4,128,256]{3,2,1,0:T(8,128)(2,1)S(1)} custom-call(bf16[128,1024]{1,0:T(8,128)(2,1)S(1)} %bitcast.41), custom_call_target="tpu_custom_call" | custom-call | tf_op jit(solution)/shard_map/pallas_call | solution.py:300
  83.1 13.6 %shard_map.96 = (bf16[512,1024]{1,0:T(8,128)(2,1)S(1)}, bf16[1024,256]{1,0:T(8,128)(2,1)S(1)}) custom-call(s32[1]{0:T(128)} %bitcast.u_ref, s32[1,512]{1,0:T(1,128)S(1)} %bitcast.49, bf16[512,1024]{1,0:T(8,128)(2,1)S(1)} %bitcast.43, bf16[512,1024]{1,0:T(8,128)(2,1)S(1)} %bitcast.44, bf16[1024,256]{1,0:T(8,128)(2,1)S(1)} %bitcast.36), custom_call_target="tpu_custom_call" | custom-call | tf_op jit(solution)/shard_map/pallas_call | solution.py:356
  96.7 30.9 %shard_map.97 = (bf16[4,128,1024]{2,1,0:T(8,128)(2,1)S(1)}, bf16[128,4096]{1,0:T(8,128)(2,1)S(1)}) custom-call(bf16[2,4,128,256]{3,2,1,0:T(8,128)(2,1)S(1)} %bitcast.48, bf16[4,128,1024]{2,1,0:T(8,128)(2,1)S(1)} %bitcast.46, f32[128,128]{1,0:T(8,128)S(1)} %get-tuple-element.34.cosine, f32[128,128]{1,0:T(8,128)S(1)} %get-tuple-element.35.sine), custom_call_target="tpu_custom_call" | custom-call | tf_op jit(solution)/shard_map/pallas_call | solution.py:425
  127.6 1.3 fusion.1
  128.9 0.3 copy-done.7
  129.2 2.6 %add_convert_fusion = bf16[512,2048]{1,0:T(8,128)(2,1)} fusion(f32[512,2048]{1,0:T(8,128)S(1)} %fusion.1, bf16[2048,512]{1,0:T(8,128)(2,1)S(1)} %bitcast.54, bf16[512,1024]{1,0:T(8,128)(2,1)S(1)} %bitcast.39), kind=kOutput, calls=%fused_computation.2 | convolution fusion | flops 1075838976 | bytes 8912896 | tf_op jit(solution)/shard_map/dot_general | solution.py:545
  131.8 4.3 %bitcast_convert_fusion = bf16[2048,1024]{1,0:T(8,128)(2,1)} fusion(bf16[4,128,2048]{2,1,0:T(8,128)(2,1)S(1)} %copy-done.6, bf16[4,128,1024]{2,1,0:T(8,128)(2,1)S(1)} %get-tuple-element.27), kind=kOutput, calls=%fused_computation | convolution fusion | flops 2149580800 | bytes 7340032 | tf_op jit(solution)/shard_map/dot_general | solution.py:548
  136.2 38.2 %shard_map.98 = (bf16[128,8192]{1,0:T(8,128)(2,1)S(1)}, bf16[16,64,1024]{2,1,0:T(8,128)(2,1)S(1)}) custom-call(bf16[4,128,2048]{2,1,0:T(8,128)(2,1)} %bitcast.51, bf16[2,4,2,2,64,1024]{5,4,3,2,1,0:T(8,128)(2,1)} %bitcast.52), custom_call_target="tpu_custom_call" | custom-call | tf_op jit(solution)/shard_map/pallas_call | solution.py:506
  174.3 0.4 convert_reduce_fusion
  174.7 0.7 fusion.7
  175.4 1.0 copy.16
  176.4 1.3 copy.17
  (21 shorter events, 0.2 us)
Async XLA Ops:
  2.8 1.2 copy-start
  4.0 0.8 copy-start.3
  4.9 0.8 copy-start.4
  41.0 3.7 %copy-start.5 = (bf16[4,128,2048]{2,1,0:T(8,128)(2,1)}, bf16[4,128,2048]{2,1,0:T(8,128)(2,1)S(1)}, u32[]{:S(2)}) copy-start(bf16[4,128,2048]{2,1,0:T(8,128)(2,1)S(1)} %get-tuple-element.18) | copy-start | bytes 6291460
  41.0 3.7 %copy-start.8 = (bf16[2,4,2,2,64,512]{5,4,3,2,1,0:T(8,128)(2,1)S(1)}, bf16[2,4,2,2,64,512]{5,4,3,2,1,0:T(8,128)(2,1)}, u32[]{:S(2)}) copy-start(bf16[2,4,2,2,64,512]{5,4,3,2,1,0:T(8,128)(2,1)} %get-tuple-element.19) | copy-start | bytes 6291460
  44.6 1.3 copy-start.1
  67.4 0.8 copy-start.2
  70.1 0.9 copy-start.10
  83.1 44.6 %copy-start.9 = (bf16[2,4,2,2,64,512]{5,4,3,2,1,0:T(8,128)(2,1)S(1)}, bf16[2,4,2,2,64,512]{5,4,3,2,1,0:T(8,128)(2,1)}, u32[]{:S(2)}) copy-start(bf16[2,4,2,2,64,512]{5,4,3,2,1,0:T(8,128)(2,1)} %get-tuple-element.19) | copy-start | bytes 6291460
  127.6 1.6 copy-start.7
  129.2 2.6 %copy-start.6 = (bf16[4,128,2048]{2,1,0:T(8,128)(2,1)S(1)}, bf16[4,128,2048]{2,1,0:T(8,128)(2,1)}, u32[]{:S(2)}) copy-start(bf16[4,128,2048]{2,1,0:T(8,128)(2,1)} %copy-done.5) | copy-start | bytes 6291460

commit v2 on v0

v2 whole, which is shorter than its diff:
```python
import functools

import jax
import jax.numpy as jnp
from jax import lax
from jax.experimental import pallas as pl
from jax.experimental.pallas import tpu as pltpu
from jax.sharding import PartitionSpec as P

KV_HEADS = 4
HD = 128
ROPE_BASE = 500000.0
NEGATIVE = -1e30
LOG2E = 1.4426950408889634
MESH = pl.DeviceIdType.MESH
TOK = 128
WIDE = 8192
ANY = pl.BlockSpec(memory_space=pl.ANY)
VMEM = pl.BlockSpec(memory_space=pltpu.VMEM)
BF = jnp.bfloat16
F32 = jnp.float32


def own_tables(lengths, offset):
    at = offset + lax.broadcasted_iota(jnp.int32, (TOK, HD), 0)
    first, second = lengths[0], lengths[0] + lengths[1]
    begin = jnp.where(at >= second, second, jnp.where(at >= first, first, 0))
    lane = lax.broadcasted_iota(jnp.int32, (TOK, HD), 1)
    frequency = ROPE_BASE ** (-2.0 * (lane % (HD // 2)).astype(F32) / HD)
    angles = (at - begin).astype(F32) * frequency
    return jnp.cos(angles), jnp.where(lane < HD // 2, -1.0, 1.0) * jnp.sin(angles)


def place():
    j, i = lax.axis_index("zero"), lax.axis_index("dp")
    return j // 4, j % 4, i // 4, (i // 2) % 2, i % 2


def device(u, x, z, w, c):
    return (u * 4 + x, z * 4 + w * 2 + c)


class Peers:
    def __init__(self):
        self.u, self.x, self.z, self.w, self.c = place()

    def along_x(self, d):
        return device(self.u, (self.x + d) % 4, self.z, self.w, self.c)

    def along_z(self, d):
        return device(self.u, self.x, (self.z + d) % 4, self.w, self.c)

    def y_at(self, d):
        y = (2 * self.u + self.w + d) % 4
        return y // 2, y % 2

    def along_y(self, d):
        u, w = self.y_at(d)
        return device(u, self.x, self.z, w, self.c)

    def in_group(self, du, dx):
        return device((self.u + du) % 2, (self.x + dx) % 4, self.z, self.w, self.c)

    def on_plane(self, dy, dx):
        u, w = self.y_at(dy)
        return device(u, (self.x + dx) % 4, self.z, w, self.c)

    def sibling(self):
        return device(self.u, self.x, self.z, self.w, 1 - self.c)


def meet(devices):
    barrier = pltpu.get_barrier_semaphore()
    for one in devices:
        pl.semaphore_signal(barrier, inc=1, device_id=one, device_id_type=MESH)
    pl.semaphore_wait(barrier, len(devices))


class Copies:
    def __init__(self, send, recv):
        self.send, self.recv, self.used = send, recv, 0

    def make(self, src, dst, to):
        at = self.used
        self.used += 1
        return pltpu.make_async_remote_copy(
            src_ref=src,
            dst_ref=dst,
            send_sem=self.send.at[at],
            recv_sem=self.recv.at[at],
            device_id=to,
            device_id_type=MESH,
        )

    def start(self, src, dst, to):
        copy = self.make(src, dst, to)
        copy.start()
        return copy


GROUP = [(du, dx) for du in (1, 0) for dx in (2, 1, 3, 0)][:-1]
PLANE = [(dy, dx) for dy in (2, 1, 3, 0) for dx in (2, 1, 3, 0)][:-1]
STEPS = (1, 3, 2)


def comm_call(kernel, number, outs, in_specs, out_specs, remote, local, scratch=()):
    return pl.pallas_call(
        kernel,
        out_shape=outs,
        in_specs=in_specs,
        out_specs=out_specs,
        scratch_shapes=[
            pltpu.SemaphoreType.DMA((remote,)),
            pltpu.SemaphoreType.DMA((remote,)),
            pltpu.SemaphoreType.DMA((local,)),
            *scratch,
        ],
        compiler_params=pltpu.CompilerParams(
            collective_id=number, has_side_effects=True, vmem_limit_bytes=60 << 20
        ),
    )


def lanes(at, size):
    return pl.ds(pl.multiple_of(at * size, size), size)


def turn(rows):
    return pltpu.roll(rows, HD // 2, 1)


def forward_kernel(
    hidden, query, grad, wkey, wvalue, cosine, sine,
    hid_out, wk_out, wv_out, q_h, go_h, kv_h,
    send, recv, here, hid, wk, wv, k_part, v_part, k_in, v_in, k_own, v_own, kv,
):
    p = Peers()
    u, x, z, w, c = p.u, p.x, p.z, p.w, p.c
    cp = Copies(send, recv)
    used = [0]

    def move(src, dst):
        copy = pltpu.make_async_copy(src, dst, here.at[used[0]])
        used[0] += 1
        copy.start()
        return copy

    own_key = move(wkey, wk.at[u, x, w, c])
    own_value = move(wvalue, wv.at[u, x, w, c])
    own_hidden = [
        move(hidden.at[:, lanes(piece * 4 + z, 256)], hid.at[z, :, pl.ds(piece * 256, 256)])
        for piece in range(8)
    ]
    later = [
        move(query.at[:, lanes(x, 1024)], q_h.at[x]),
        move(grad.at[:, lanes(x, 1024)], go_h.at[x]),
    ]
    meet(
        [p.along_z(d) for d in STEPS]
        + [p.on_plane(dy, 0) for dy in STEPS]
        + [p.on_plane(0, dx) for dx in STEPS]
        + [p.on_plane(2, dx) for dx in STEPS]
        + [p.sibling()]
    )
    key_y = [cp.start(wkey, wk.at[u, x, w, c], p.along_y(d)) for d in STEPS]
    value_x = [cp.start(wvalue, wv.at[u, x, w, c], p.along_x(d)) for d in STEPS]
    whole = []
    for d in STEPS:
        there, at = (z + d) % 4, cp.used
        for piece in range(8):
            cp.used = at
            cp.start(
                hidden.at[:, lanes(piece * 4 + there, 256)],
                hid.at[z, :, pl.ds(piece * 256, 256)],
                p.along_z(d),
            )
        cp.used = at
        came = (z + 4 - d) % 4
        whole.append(cp.make(hid.at[came], hid.at[came], p.along_z(d)))
    own_key.wait()
    for one in key_y:
        one.wait_recv()
    column = wk.at[:, x, :, c]
    key_x = [cp.start(column, column, p.along_x(d)) for d in STEPS]
    to_core = [cp.start(column, column, p.sibling())]
    own_value.wait()
    for one in value_x:
        one.wait_recv()
    row = wv.at[u, :, w, c]
    value_y = [cp.start(row, row, p.along_y(d)) for d in STEPS]
    to_core.append(cp.start(row, row, p.sibling()))
    sent = []
    for source, target in ((query, q_h), (grad, go_h)):
        for d in STEPS:
            sent.append(
                cp.start(source.at[:, lanes((x + d) % 4, 1024)], target.at[x], p.along_x(d))
            )
    for d, one in zip(STEPS, key_x):
        one.wait_recv()
        column = wk.at[:, (x + 4 - d) % 4, :, c]
        to_core.append(cp.start(column, column, p.sibling()))
    for d, one in zip(STEPS, value_y):
        one.wait_recv()
        from_u, from_w = p.y_at(4 - d)
        row = wv.at[from_u, :, from_w, c]
        to_core.append(cp.start(row, row, p.sibling()))
    for one in own_hidden:
        one.wait()
    for one in to_core:
        one.wait_recv()
    later += [move(wk, wk_out), move(wv, wv_out), move(hid.at[z], hid_out.at[z])]

    def project(slot, weights):
        return jnp.dot(hid[slot], weights[...].reshape(2048, 512), preferred_element_type=F32)

    k_own[...] = project(z, wk)
    v_own[...] = project(z, wv)
    back = []
    for number, d in enumerate(STEPS):
        slot = (z + 4 - d) % 4
        whole[number].wait_recv()
        later.append(move(hid.at[slot], hid_out.at[slot]))
        k_part[number] = project(slot, wk)
        back.append(cp.start(k_part.at[number], k_in.at[number], p.along_z(4 - d)))
        v_part[number] = project(slot, wv).astype(BF)
        back.append(cp.start(v_part.at[number], v_in.at[number], p.along_z(4 - d)))
    for one in back:
        one.wait_recv()
    cos, sin = cosine[...], sine[...]
    for h in range(KV_HEADS):
        part = slice(h * HD, (h + 1) * HD)
        k, v = k_own[:, part], v_own[:, part]
        for number in range(3):
            k = k + k_in[number, :, part]
            v = v + v_in[number, :, part].astype(F32)
        kv[:, 2 * h * HD : (2 * h + 1) * HD] = (k * cos + turn(k) * sin).astype(BF)
        kv[:, (2 * h + 1) * HD : (2 * h + 2) * HD] = v.astype(BF)
    later.append(move(kv.at[:, lanes(x, 256)], kv_h.at[u, x]))
    sent += [
        cp.start(kv.at[:, lanes((x + dx) % 4, 256)], kv_h.at[u, x], p.in_group(du, dx))
        for du, dx in GROUP
    ]
    for one in sent:
        one.wait_recv()
    for one in key_y + value_x + whole + key_x + value_y + to_core + back + sent:
        one.wait_send()
    for one in later:
        one.wait()


def forward(hidden, query, grad, wkey, wvalue, cosine, sine):
    shape = jax.ShapeDtypeStruct
    weights = (2, 4, 2, 2, 64, 512)
    return comm_call(
        forward_kernel,
        0,
        (
            shape((4, TOK, 2048), BF),
            shape(weights, BF),
            shape(weights, BF),
            shape((4, TOK, 1024), BF),
            shape((4, TOK, 1024), BF),
            shape((2, 4, TOK, 256), BF),
        ),
        [ANY] * 5 + [VMEM] * 2,
        (ANY,) * 6,
        42,
        19,
        (
            pltpu.VMEM((4, TOK, 2048), BF),
            pltpu.VMEM(weights, BF),
            pltpu.VMEM(weights, BF),
            pltpu.VMEM((3, TOK, 512), F32),
            pltpu.VMEM((3, TOK, 512), BF),
            pltpu.VMEM((3, TOK, 512), F32),
            pltpu.VMEM((3, TOK, 512), BF),
            pltpu.VMEM((TOK, 512), F32),
            pltpu.VMEM((TOK, 512), F32),
            pltpu.VMEM((TOK, 1024), BF),
        ),
    )(hidden, query, grad, wkey, wvalue, cosine, sine)


ROWS = 256


def attend_kernel(scalars, q, go, kv, dq, dkv, bias, kt, dk_sum, dv_sum):
    u = scalars[0]
    first, second = scalars[1], scalars[1] + scalars[2]
    scale = HD**-0.5
    contract = (((1,), (1,)), ((), ()))
    dk_sum[...] = jnp.zeros_like(dk_sum)
    dv_sum[...] = jnp.zeros_like(dv_sum)
    kt[...] = kv[:, :HD].astype(F32).T.astype(BF)

    def work(block, keys):
        at = slice(block * ROWS, (block + 1) * ROWS)
        key_at = lax.broadcasted_iota(jnp.int32, (keys, ROWS), 0)
        query_at = keys - ROWS + lax.broadcasted_iota(jnp.int32, (1, ROWS), 1)
        begin = jnp.where(query_at >= second, second, jnp.where(query_at >= first, first, 0))
        allowed = (key_at <= query_at) & (key_at >= begin)
        bias[:keys] = jnp.where(allowed, 0.0, NEGATIVE)

        def one_head(head, carry):
            query, grad = q[at, lanes(head, HD)], go[at, lanes(head, HD)]
            key, value = kv[:keys, :HD], kv[:keys, HD:]
            s = lax.dot_general(key, query, contract, preferred_element_type=F32) + bias[:keys]
            top = jnp.max(s, axis=0, keepdims=True)
            e = jnp.exp2((s - top) * (scale * LOG2E))
            weights = e * (1.0 / jnp.sum(e, axis=0, keepdims=True))
            low = weights.astype(BF)
            dw = lax.dot_general(value, grad, contract, preferred_element_type=F32)
            delta = jnp.sum(low.astype(F32) * dw, axis=0, keepdims=True)
            ds = (weights * (dw - delta)).astype(BF)
            dv_sum[:keys] += jnp.dot(low, grad, preferred_element_type=F32)
            dk_sum[:keys] += jnp.dot(ds, query, preferred_element_type=F32)
            turned = jnp.dot(kt[:, :keys], ds, preferred_element_type=F32)
            dq[at, lanes(head, HD)] = (turned.T * scale).astype(BF)
            return carry

        lax.fori_loop(0, 8, one_head, 0)

    for half in range(2):
        for block in range(2):
            pl.when(u == half)(functools.partial(work, block, (half * 2 + block + 1) * ROWS))
    dkv[:, :HD] = (dk_sum[...] * scale).astype(BF)
    dkv[:, HD:] = dv_sum[...].astype(BF)


def attend(scalars, q_h, go_h, kv_h):
    shape = jax.ShapeDtypeStruct
    return pl.pallas_call(
        attend_kernel,
        in_specs=[pl.BlockSpec(memory_space=pltpu.SMEM), VMEM, VMEM, VMEM],
        out_specs=[VMEM, VMEM],
        scratch_shapes=[
            pltpu.VMEM((1024, ROWS), F32),
            pltpu.VMEM((HD, 1024), BF),
            pltpu.VMEM((1024, HD), F32),
            pltpu.VMEM((1024, HD), F32),
        ],
        out_shape=[shape((512, 1024), BF), shape((1024, 256), BF)],
        compiler_params=pltpu.CompilerParams(vmem_limit_bytes=56 << 20),
    )(scalars, q_h, go_h, kv_h)


def backward_kernel(
    dkv, dq_h, hid_in, wk_in, wv_in, cosine, sine,
    dq, dhidden, grad_key, grad_value,
    send, recv, here, came, rows, hid, turned, wk, wv, dh, mine, low, away, other, terms,
):
    p = Peers()
    u, x, z, w, c = p.u, p.x, p.z, p.w, p.c
    cp = Copies(send, recv)
    used = [0]

    def move(src, dst):
        copy = pltpu.make_async_copy(src, dst, here.at[used[0]])
        used[0] += 1
        copy.start()
        return copy

    hid_load = move(hid_in, hid)
    first = move(dkv.at[u, x], came.at[u, x])
    weight_loads = [move(wk_in, wk), move(wv_in, wv)]
    later = [move(dq_h.at[x], dq.at[:, lanes(x, 1024)])]
    meet(
        [p.along_z(d) for d in STEPS]
        + [p.on_plane(dy, dx) for dy, dx in PLANE]
        + [p.sibling()]
    )
    pieces = [
        cp.start(dkv.at[(u + du) % 2, (x + dx) % 4], came.at[u, x], p.in_group(du, dx))
        for du, dx in GROUP
    ]
    hid_load.wait()

    def transpose(k, carry):
        block = hid[:, :, lanes(k, 128)].reshape(512, 128)
        turned[k] = block.astype(F32).T.astype(BF)
        return carry

    lax.fori_loop(0, 16, transpose, 0)
    first.wait()
    for one in pieces:
        one.wait_recv()
    cos, sin = cosine[...], sine[...]
    for h in range(KV_HEADS):
        total = came[0, h].astype(F32) + came[1, h].astype(F32)
        dk = total[:, :HD]
        rows[z, :, h * HD : (h + 1) * HD] = (dk * cos - turn(dk) * sin).astype(BF)
        rows[z, :, 512 + h * HD : 512 + (h + 1) * HD] = total[:, HD:].astype(BF)
    sent_z = [cp.start(rows.at[z], rows.at[z], p.along_z(d)) for d in STEPS]
    sent = [
        cp.start(dq_h.at[(x + d) % 4], dq.at[:, lanes(x, 1024)], p.along_x(d)) for d in STEPS
    ]
    for one in weight_loads:
        one.wait()
    contract = (((1,), (1,)), ((), ()))

    def hidden_rows(slot, number):
        def one(piece, carry):
            key = wk[piece // 4, piece % 4].reshape(256, 512)
            value = wv[piece // 4, piece % 4].reshape(256, 512)
            total = lax.dot_general(
                rows[slot, :, :512], key, contract, preferred_element_type=F32
            ) + lax.dot_general(rows[slot, :, 512:], value, contract, preferred_element_type=F32)
            dh[number, :, lanes(piece, 256)] = total.astype(BF)
            return carry

        lax.fori_loop(0, 8, one, 0)

    hidden_rows(z, 3)
    for piece in range(8):
        later.append(
            move(
                dh.at[3, :, pl.ds(piece * 256, 256)],
                dhidden.at[:, lanes(piece * 4 + z, 256)],
            )
        )
    whole = []
    for number, d in enumerate(STEPS):
        slot = (z + 4 - d) % 4
        sent_z[number].wait_recv()
        hidden_rows(slot, number)
        at = cp.used
        for piece in range(8):
            cp.used = at
            cp.start(
                dh.at[number, :, pl.ds(piece * 256, 256)],
                dhidden.at[:, lanes(piece * 4 + z, 256)],
                p.along_z(4 - d),
            )
        cp.used = at
        whole.append(cp.make(dh.at[number], dh.at[number], p.along_z(4 - d)))
    order = PLANE + [(0, 0)]
    swapped, out = [], []

    def pass_on(k):
        swapped[k].wait_recv()
        low[k] = (mine[k] + other[k].astype(F32)).astype(BF)
        dy, dx = order[k]
        if k < 15:
            out.append(cp.start(low.at[k], terms.at[k], p.on_plane(dy, dx)))

    for k, (dy, dx) in enumerate(order):
        tu, tw = p.y_at(dy)
        block = (tu * 4 + (x + dx) % 4) * 2 + tw
        product = jnp.dot(
            turned[block], rows[...].reshape(512, 1024), preferred_element_type=F32
        )
        zero_core = c == 0
        mine[k] = jnp.where(zero_core, product[:64], product[64:])
        away[k] = jnp.where(zero_core, product[64:], product[:64]).astype(BF)
        swapped.append(cp.start(away.at[k], other.at[k], p.sibling()))
        if k >= 2:
            pass_on(k - 2)
    pass_on(14)
    pass_on(15)
    for one in out:
        one.wait_recv()
    total = low[15].astype(F32)
    for k in range(15):
        total = total + terms[k].astype(F32)
    grad_key[...] = total[:, :512]
    grad_value[...] = total[:, 512:]
    for one in whole + sent:
        one.wait_recv()
    for one in pieces + sent_z + sent + whole + swapped + out:
        one.wait_send()
    for one in later:
        one.wait()


def backward(dkv, dq_h, hid_g, wk, wv, cosine, sine):
    shape = jax.ShapeDtypeStruct
    weights = (2, 4, 2, 2, 64, 512)
    return comm_call(
        backward_kernel,
        1,
        (
            shape((TOK, 4096), BF),
            shape((TOK, WIDE), BF),
            shape((64, 512), F32),
            shape((64, 512), F32),
        ),
        [ANY] * 5 + [VMEM] * 2,
        (ANY, ANY, VMEM, VMEM),
        7 + 3 + 3 + 3 + 16 + 15,
        13,
        (
            pltpu.VMEM((2, 4, TOK, 256), BF),
            pltpu.VMEM((4, TOK, 1024), BF),
            pltpu.VMEM((4, TOK, 2048), BF),
            pltpu.VMEM((16, TOK, 512), BF),
            pltpu.VMEM(weights, BF),
            pltpu.VMEM(weights, BF),
            pltpu.VMEM((4, TOK, 2048), BF),
            pltpu.VMEM((16, 64, 1024), F32),
            pltpu.VMEM((16, 64, 1024), BF),
            pltpu.VMEM((16, 64, 1024), BF),
            pltpu.VMEM((16, 64, 1024), BF),
            pltpu.VMEM((15, 64, 1024), BF),
        ),
    )(dkv, dq_h, hid_g, wk, wv, cosine, sine)


def local(hidden, queries, grad_out, key_weight, value_weight, doc_lengths):
    lengths = doc_lengths[0]
    zero = lax.axis_index("zero")
    cosine, sine = own_tables(lengths, zero * TOK)
    hid_g, wk, wv, q_h, go_h, kv_h = forward(
        hidden[0], queries[0], grad_out[0], key_weight, value_weight, cosine, sine
    )
    scalars = jnp.concatenate([(zero // 4).astype(jnp.int32)[None], lengths])
    dq_h, dkv = attend(
        scalars, q_h.reshape(512, 1024), go_h.reshape(512, 1024), kv_h.reshape(1024, 256)
    )
    dquery, dhidden, grad_key, grad_value = backward(
        dkv.reshape(2, 4, TOK, 256), dq_h.reshape(4, TOK, 1024), hid_g, wk, wv, cosine, sine
    )
    return dquery[None], dhidden[None], grad_key, grad_value


def solution(mesh):
    return jax.shard_map(
        local,
        mesh=mesh,
        in_specs=(
            P("dp", "zero", None),
            P("dp", "zero", None),
            P("dp", "zero", None),
            P(("zero", "dp"), None),
            P(("zero", "dp"), None),
            P("dp", None),
        ),
        out_specs=(
            P("dp", "zero", None),
            P("dp", "zero", None),
            P(("zero", "dp"), None),
            P(("zero", "dp"), None),
        ),
        check_vma=False,
    )
```

time: 1070 us -> 164 us (0.15)
  waiting for transfers between devices: 922 us -> 0 us
  Pallas kernels: 0 us -> 151 us
  matrix products: 85.6 us -> 0 us
  local copies, waits for them, and re-layouts: 33.5 us -> 6.39 us
  other arithmetic: 15.4 us -> 2.98 us
  between operations: 14.4 us -> 2 us
    all_gather x4 -> x0, waiting for transfers between devices: 459 us -> none  [the longest x1 203 us: local(): lax.all_gather(key_weight, ('zero', 'dp'), axis=0, tiled=True)]
    unnamed x14 -> x0, waiting for transfers between devices: 240 us -> none
    reduce_scatter x2 -> x0, waiting for transfers between devices: 224 us -> none  [the longest x1 114 us: local(): lax.psum_scatter(value_terms.astype(jnp.bfloat16), 'zero', scatter_dimens...]
    pallas_call x0 -> x3, Pallas kernels: none -> 151 us  [the longest x1 78 us: backward(): comm_call(backward_kernel, 1, (shape((TOK, 4096), BF), shape((TOK, WIDE),...]
    dot_general x12 -> x0, matrix products: 85.6 us -> none  [the longest x1 11.9 us: output_work(): jnp.einsum('kgts,skd->kgtd', weights, value_block, preferred_element_type...]
    unnamed x27 -> x10, local copies, waits for them, and re-layouts: 16.8 us -> 5.08 us
    dot_general x2 -> x0, local copies, waits for them, and re-layouts: 11.4 us -> none  [the longest x1 11.3 us: local(): jnp.dot(rows_in, full_key, preferred_element_type=jnp.float32)]
  transfers between devices with their start and end apart: 10 -> 0, of which waited for: 10 -> 0; matrix products, arithmetic and copies ran while one was open for 9% -> 0% of each run, Pallas kernels for 0% -> 0%
where the time goes in v2:
time: 164 us; the launch traced here: 163 us
  Pallas kernels  151 us (92%)
  local copies, waits for them, and re-layouts  6.39 us (4%)
  other arithmetic  2.98 us (2%)
  between operations  2 us (1%)
    pallas_call x1, Pallas kernels, backward(): comm_call(backward_kernel, 1, (shape((TOK, 4096), BF), shape((TOK, WIDE),...  78 us
    pallas_call x1, Pallas kernels, forward(): comm_call(forward_kernel, 0, (shape((4, TOK, 2048), BF), shape(weights, B...  58.5 us
    pallas_call x1, Pallas kernels, attend(): pl.pallas_call(attend_kernel, in_specs=[pl.BlockSpec(memory_space=pltpu.S...  14.9 us
    unnamed x10, local copies, waits for them, and re-layouts  5.08 us

profile of v2, /device:TPU:6, one launch (start us, length us, event | category | flops | bytes accessed | tf_op | source)
XLA Modules:
  0.0 162.8 jit_solution(3710199823121337329)
XLA Ops:
  0.6 1.3 pad_add_fusion.scalars
  2.0 1.3 fusion.1
  4.6 0.6 compare_select_fusion.1
  5.3 1.0 sine_multiply_fusion
  6.3 58.5 %shard_map.93 = (bf16[4,128,2048]{2,1,0:T(8,128)(2,1)}, bf16[2,4,2,2,64,512]{5,4,3,2,1,0:T(8,128)(2,1)}, bf16[2,4,2,2,64,512]{5,4,3,2,1,0:T(8,128)(2,1)}, bf16[4...) custom-call(bf16[128,8192]{1,0:T(8,128)(2,1)} %bitcast.14, ...), custom_call_target="tpu_custom_call" | custom-call | tf_op jit(solution)/shard_map/pallas_call | solution.py:254
  64.8 14.9 %shard_map.94 = (bf16[512,1024]{1,0:T(8,128)(2,1)}, bf16[1024,256]{1,0:T(8,128)(2,1)}) custom-call(s32[4]{0:T(128)} %pad_add_fusion.scalars, bf16[512,1024]{1,0:T(8,128)(2,1)} %bitcast.20, bf16[512,1024]{1,0:T(8,128)(2,1)} %bitcast.21, bf16[1024,256]{1,0:T(8,128)(2,1)} %bitcast.22), custom_call_target="tpu_custom_call" | custom-call | tf_op jit(solution)/shard_map/pallas_call | solution.py:332
  79.7 78.0 %shard_map.95 = (bf16[128,4096]{1,0:T(8,128)(2,1)}, bf16[128,8192]{1,0:T(8,128)(2,1)}, f32[64,512]{1,0:T(8,128)}, f32[64,512]{1,0:T(8,128)}) custom-call(bf16[2,4,128,256]{3,2,1,0:T(8,128)(2,1)} %bitcast.23, bf16[4,128,1024]{2,1,0:T(8,128)(2,1)} %bitcast.18, bf16[4,128,2048]{2,1,0:T(8,128)(2,1)} %get-tuple-element.21.hid_in, ...), custom_call_target="tpu_custom_call" | custom-call | tf_op jit(solution)/shard_map/pallas_call | solution.py:478
  157.7 0.0 copy-start
  157.7 2.4 %copy.14 = bf16[1,128,4096]{2,1,0:T(8,128)(2,1)} copy(bf16[1,128,4096]{2,1,0:T(8,128)(2,1)} %bitcast.19) | data formatting | bytes 2097152
  160.2 0.0 copy-done
  160.2 0.0 copy-start.2
  160.2 0.0 copy-start.1
  160.2 1.3 copy.15
  161.5 0.0 copy-done.2
  161.5 0.7 copy.16
  162.1 0.0 copy-done.1
  162.2 0.7 copy.17
  (3 shorter events, 0.0 us)
Async XLA Ops:
  157.7 2.4 %copy-start = (bf16[128,8192]{1,0:T(8,128)(2,1)S(1)}, bf16[128,8192]{1,0:T(8,128)(2,1)}, u32[]{:S(2)}) copy-start(bf16[128,8192]{1,0:T(8,128)(2,1)} %get-tuple-element.25) | copy-start | bytes 6291460
  160.2 1.3 copy-start.2
  160.2 2.0 %copy-start.1 = (f32[64,512]{1,0:T(8,128)S(1)}, f32[64,512]{1,0:T(8,128)}, u32[]{:S(2)}) copy-start(f32[64,512]{1,0:T(8,128)} %get-tuple-element.45) | copy-start | bytes 393220

commit v3 on v2

--- a/solution.py
+++ b/solution.py
@@ -236,12 +236,33 @@
         kv[:, 2 * h * HD : (2 * h + 1) * HD] = (k * cos + turn(k) * sin).astype(BF)
         kv[:, (2 * h + 1) * HD : (2 * h + 2) * HD] = v.astype(BF)
     later.append(move(kv.at[:, lanes(x, 256)], kv_h.at[u, x]))
+    across = [
+        cp.make(kv.at[:, lanes((x + dx) % 4, 256)], kv_h.at[u, x], p.in_group(1, dx))
+        for dx in (2, 1, 3, 0)
+    ]
+
+    @pl.when(u == 0)
+    def _():
+        for one in across:
+            one.start()
+
     sent += [
-        cp.start(kv.at[:, lanes((x + dx) % 4, 256)], kv_h.at[u, x], p.in_group(du, dx))
-        for du, dx in GROUP
+        cp.start(kv.at[:, lanes((x + dx) % 4, 256)], kv_h.at[u, x], p.along_x(dx))
+        for dx in STEPS
     ]
     for one in sent:
         one.wait_recv()
+
+    @pl.when(u == 0)
+    def _():
+        for one in across:
+            one.wait_send()
+
+    @pl.when(u == 1)
+    def _():
+        for one in across:
+            one.wait_recv()
+
     for one in key_y + value_x + whole + key_x + value_y + to_core + back + sent:
         one.wait_send()
     for one in later:
@@ -347,7 +368,8 @@
 def backward_kernel(
     dkv, dq_h, hid_in, wk_in, wv_in, cosine, sine,
     dq, dhidden, grad_key, grad_value,
-    send, recv, here, came, rows, hid, turned, wk, wv, dh, mine, low, away, other, terms,
+    send, recv, here, came, rows, hid, turned, wk, wv, dh, mine, low, away, other,
+    key_in, value_in, key_sum, value_sum, key_last, value_last,
 ):
     p = Peers()
     u, x, z, w, c = p.u, p.x, p.z, p.w, p.c
@@ -369,9 +391,19 @@
         + [p.on_plane(dy, dx) for dy, dx in PLANE]
         + [p.sibling()]
     )
+    across = [
+        cp.make(dkv.at[0, (x + dx) % 4], came.at[1, x], p.in_group(1, dx))
+        for dx in (2, 1, 3, 0)
+    ]
+
+    @pl.when(u == 1)
+    def _():
+        for one in across:
+            one.start()
+        came[0] = jnp.zeros((4, TOK, 256), BF)
+
     pieces = [
-        cp.start(dkv.at[(u + du) % 2, (x + dx) % 4], came.at[u, x], p.in_group(du, dx))
-        for du, dx in GROUP
+        cp.start(dkv.at[u, (x + dx) % 4], came.at[u, x], p.along_x(dx)) for dx in STEPS
     ]
     hid_load.wait()
 
@@ -384,6 +416,17 @@
     first.wait()
     for one in pieces:
         one.wait_recv()
+
+    @pl.when(u == 0)
+    def _():
+        for one in across:
+            one.wait_recv()
+
+    @pl.when(u == 1)
+    def _():
+        for one in across:
+            one.wait_send()
+
     cos, sin = cosine[...], sine[...]
     for h in range(KV_HEADS):
         total = came[0, h].astype(F32) + came[1, h].astype(F32)
@@ -434,14 +477,21 @@
         cp.used = at
         whole.append(cp.make(dh.at[number], dh.at[number], p.along_z(4 - d)))
     order = PLANE + [(0, 0)]
-    swapped, out = [], []
+    y = 2 * u + w
+    swapped, key_out, value_out = [], {}, {}
 
     def pass_on(k):
         swapped[k].wait_recv()
         low[k] = (mine[k] + other[k].astype(F32)).astype(BF)
         dy, dx = order[k]
-        if k < 15:
-            out.append(cp.start(low.at[k], terms.at[k], p.on_plane(dy, dx)))
+        if dx:
+            key_out[dy, dx] = cp.start(
+                low.at[k, :, pl.ds(0, 512)], key_in.at[dx - 1, (y + dy) % 4], p.along_x(dx)
+            )
+        if dy:
+            value_out[dy, dx] = cp.start(
+                low.at[k, :, pl.ds(512, 512)], value_in.at[dy - 1, (x + dx) % 4], p.along_y(dy)
+            )
 
     for k, (dy, dx) in enumerate(order):
         tu, tw = p.y_at(dy)
@@ -457,13 +507,36 @@
             pass_on(k - 2)
     pass_on(14)
     pass_on(15)
-    for one in out:
-        one.wait_recv()
-    total = low[15].astype(F32)
-    for k in range(15):
-        total = total + terms[k].astype(F32)
-    grad_key[...] = total[:, :512]
-    grad_value[...] = total[:, 512:]
+    last = []
+    for d in (2, 1, 3, 0):
+        for one in range(1, 4):
+            key_out[d, one].wait_recv()
+        at = order.index((d, 0))
+        total = low[at, :, :512].astype(F32)
+        for one in range(3):
+            total = total + key_in[one, (y + d) % 4].astype(F32)
+        if d:
+            key_sum[d - 1] = total.astype(BF)
+            last.append(cp.start(key_sum.at[d - 1], key_last.at[d - 1], p.along_y(d)))
+        else:
+            grad_key[...] = total
+        for one in range(1, 4):
+            value_out[one, d].wait_recv()
+        at = order.index((0, d))
+        total = low[at, :, 512:].astype(F32)
+        for one in range(3):
+            total = total + value_in[one, (x + d) % 4].astype(F32)
+        if d:
+            value_sum[d - 1] = total.astype(BF)
+            last.append(cp.start(value_sum.at[d - 1], value_last.at[d - 1], p.along_x(d)))
+        else:
+            grad_value[...] = total
+    for one in last:
+        one.wait_recv()
+    for one in range(3):
+        grad_key[...] += key_last[one].astype(F32)
+        grad_value[...] += value_last[one].astype(F32)
+    out = list(key_out.values()) + list(value_out.values()) + last
     for one in whole + sent:
         one.wait_recv()
     for one in pieces + sent_z + sent + whole + swapped + out:
@@ -486,7 +559,7 @@
         ),
         [ANY] * 5 + [VMEM] * 2,
         (ANY, ANY, VMEM, VMEM),
-        7 + 3 + 3 + 3 + 16 + 15,
+        7 + 3 + 3 + 3 + 16 + 12 + 12 + 6,
         13,
         (
             pltpu.VMEM((2, 4, TOK, 256), BF),
@@ -500,7 +573,9 @@
             pltpu.VMEM((16, 64, 1024), BF),
             pltpu.VMEM((16, 64, 1024), BF),
             pltpu.VMEM((16, 64, 1024), BF),
-            pltpu.VMEM((15, 64, 1024), BF),
+            pltpu.VMEM((3, 4, 64, 512), BF),
+            pltpu.VMEM((3, 4, 64, 512), BF),
+            *[pltpu.VMEM((3, 64, 512), BF)] * 4,
         ),
     )(dkv, dq_h, hid_g, wk, wv, cosine, sine)
 

time: 164 us -> 149 us (0.909)
  Pallas kernels: 151 us -> 137 us
    pallas_call x1, Pallas kernels: 78 us -> 64.6 us  [backward(): comm_call(backward_kernel, 1, (shape((TOK, 4096), BF), shape((TOK, WIDE),...]
where the time goes in v3:
time: 149 us
  Pallas kernels  137 us (92%)
  local copies, waits for them, and re-layouts  6.39 us (4%)
  other arithmetic  2.98 us (2%)
  between operations  2 us (1%)
    pallas_call x1, Pallas kernels, backward(): comm_call(backward_kernel, 1, (shape((TOK, 4096), BF), shape((TOK, WIDE),...  64.6 us
    pallas_call x1, Pallas kernels, forward(): comm_call(forward_kernel, 0, (shape((4, TOK, 2048), BF), shape(weights, B...  58.2 us
    pallas_call x1, Pallas kernels, attend(): pl.pallas_call(attend_kernel, in_specs=[pl.BlockSpec(memory_space=pltpu.S...  14.7 us
    unnamed x10, local copies, waits for them, and re-layouts  5.08 us

profile of v3, /device:TPU:6, one launch (start us, length us, event | category | flops | bytes accessed | tf_op | source)
XLA Modules:
  0.0 148.8 jit_solution(8542215772609305652)
XLA Ops:
  0.6 1.3 pad_add_fusion.scalars
  2.0 1.3 fusion.1
  4.6 0.6 compare_select_fusion.1
  5.3 1.0 sine_multiply_fusion
  6.3 58.2 %shard_map.93 = (bf16[4,128,2048]{2,1,0:T(8,128)(2,1)}, bf16[2,4,2,2,64,512]{5,4,3,2,1,0:T(8,128)(2,1)}, bf16[2,4,2,2,64,512]{5,4,3,2,1,0:T(8,128)(2,1)}, bf16[4...) custom-call(bf16[128,8192]{1,0:T(8,128)(2,1)} %bitcast.14, ...), custom_call_target="tpu_custom_call" | custom-call | tf_op jit(solution)/shard_map/pallas_call | solution.py:275
  64.5 14.7 %shard_map.94 = (bf16[512,1024]{1,0:T(8,128)(2,1)}, bf16[1024,256]{1,0:T(8,128)(2,1)}) custom-call(s32[4]{0:T(128)} %pad_add_fusion.scalars, bf16[512,1024]{1,0:T(8,128)(2,1)} %bitcast.20, bf16[512,1024]{1,0:T(8,128)(2,1)} %bitcast.21, bf16[1024,256]{1,0:T(8,128)(2,1)} %bitcast.22), custom_call_target="tpu_custom_call" | custom-call | tf_op jit(solution)/shard_map/pallas_call | solution.py:353
  79.2 64.6 %shard_map.95 = (bf16[128,4096]{1,0:T(8,128)(2,1)}, bf16[128,8192]{1,0:T(8,128)(2,1)}, f32[64,512]{1,0:T(8,128)}, f32[64,512]{1,0:T(8,128)}) custom-call(bf16[2,4,128,256]{3,2,1,0:T(8,128)(2,1)} %bitcast.23, bf16[4,128,1024]{2,1,0:T(8,128)(2,1)} %bitcast.18, bf16[4,128,2048]{2,1,0:T(8,128)(2,1)} %get-tuple-element.21.hid_in, ...), custom_call_target="tpu_custom_call" | custom-call | tf_op jit(solution)/shard_map/pallas_call | solution.py:551
  143.8 0.0 copy-start
  143.8 2.4 %copy.14 = bf16[1,128,4096]{2,1,0:T(8,128)(2,1)} copy(bf16[1,128,4096]{2,1,0:T(8,128)(2,1)} %bitcast.19) | data formatting | bytes 2097152
  146.2 0.0 copy-done
  146.2 0.0 copy-start.2
  146.2 0.0 copy-start.1
  146.2 1.3 copy.15
  147.5 0.0 copy-done.2
  147.5 0.7 copy.16
  148.2 0.0 copy-done.1
  148.2 0.7 copy.17
  (3 shorter events, 0.0 us)
Async XLA Ops:
  143.8 2.4 %copy-start = (bf16[128,8192]{1,0:T(8,128)(2,1)S(1)}, bf16[128,8192]{1,0:T(8,128)(2,1)}, u32[]{:S(2)}) copy-start(bf16[128,8192]{1,0:T(8,128)(2,1)} %get-tuple-element.25) | copy-start | bytes 6291460
  146.2 1.3 copy-start.2
  146.2 2.0 %copy-start.1 = (f32[64,512]{1,0:T(8,128)S(1)}, f32[64,512]{1,0:T(8,128)}, u32[]{:S(2)}) copy-start(f32[64,512]{1,0:T(8,128)} %get-tuple-element.45) | copy-start | bytes 393220

commit v4 on v3

--- a/solution.py
+++ b/solution.py
@@ -2,6 +2,7 @@
 
 import jax
 import jax.numpy as jnp
+import numpy as np
 from jax import lax
 from jax.experimental import pallas as pl
 from jax.experimental.pallas import tpu as pltpu
@@ -21,14 +22,11 @@
 F32 = jnp.float32
 
 
-def own_tables(lengths, offset):
-    at = offset + lax.broadcasted_iota(jnp.int32, (TOK, HD), 0)
-    first, second = lengths[0], lengths[0] + lengths[1]
-    begin = jnp.where(at >= second, second, jnp.where(at >= first, first, 0))
-    lane = lax.broadcasted_iota(jnp.int32, (TOK, HD), 1)
-    frequency = ROPE_BASE ** (-2.0 * (lane % (HD // 2)).astype(F32) / HD)
-    angles = (at - begin).astype(F32) * frequency
-    return jnp.cos(angles), jnp.where(lane < HD // 2, -1.0, 1.0) * jnp.sin(angles)
+FREQUENCY = (ROPE_BASE ** (-2.0 * (np.arange(HD) % (HD // 2)) / HD)).astype(np.float32)
+
+
+def begin_of(at, first, second):
+    return jnp.where(at >= second, second, jnp.where(at >= first, first, 0))
 
 
 def place():
@@ -130,8 +128,8 @@
 
 
 def forward_kernel(
-    hidden, query, grad, wkey, wvalue, cosine, sine,
-    hid_out, wk_out, wv_out, q_h, go_h, kv_h,
+    hidden, query, grad, wkey, wvalue, frequency, lengths,
+    hid_out, wk_out, wv_out, q_h, go_h, kv_h, cosine, sine,
     send, recv, here, hid, wk, wv, k_part, v_part, k_in, v_in, k_own, v_own, kv,
 ):
     p = Peers()
@@ -177,6 +175,12 @@
         cp.used = at
         came = (z + 4 - d) % 4
         whole.append(cp.make(hid.at[came], hid.at[came], p.along_z(d)))
+    at = (u * 4 + x) * TOK + lax.broadcasted_iota(jnp.int32, (TOK, HD), 0)
+    begin = begin_of(at, lengths[0, 0], lengths[0, 0] + lengths[0, 1])
+    angles = (at - begin).astype(F32) * frequency[...]
+    sign = jnp.where(lax.broadcasted_iota(jnp.int32, (TOK, HD), 1) < HD // 2, -1.0, 1.0)
+    cosine[...] = jnp.cos(angles)
+    sine[...] = sign * jnp.sin(angles)
     own_key.wait()
     for one in key_y:
         one.wait_recv()
@@ -269,7 +273,7 @@
         one.wait()
 
 
-def forward(hidden, query, grad, wkey, wvalue, cosine, sine):
+def forward(hidden, query, grad, wkey, wvalue, lengths):
     shape = jax.ShapeDtypeStruct
     weights = (2, 4, 2, 2, 64, 512)
     return comm_call(
@@ -282,9 +286,11 @@
             shape((4, TOK, 1024), BF),
             shape((4, TOK, 1024), BF),
             shape((2, 4, TOK, 256), BF),
+            shape((TOK, HD), F32),
+            shape((TOK, HD), F32),
         ),
-        [ANY] * 5 + [VMEM] * 2,
-        (ANY,) * 6,
+        [ANY] * 5 + [VMEM, pl.BlockSpec(memory_space=pltpu.SMEM)],
+        (ANY,) * 6 + (VMEM,) * 2,
         42,
         19,
         (
@@ -299,56 +305,67 @@
             pltpu.VMEM((TOK, 512), F32),
             pltpu.VMEM((TOK, 1024), BF),
         ),
-    )(hidden, query, grad, wkey, wvalue, cosine, sine)
-
-
-ROWS = 256
-
-
-def attend_kernel(scalars, q, go, kv, dq, dkv, bias, kt, dk_sum, dv_sum):
-    u = scalars[0]
-    first, second = scalars[1], scalars[1] + scalars[2]
+    )(hidden, query, grad, wkey, wvalue, jnp.asarray(FREQUENCY)[None], lengths)
+
+
+ROWS = 128
+HEADS = 8
+
+
+def attend_kernel(lengths, q, go, kv, dq, dkv, bias, kt, vt, dk_sum, dv_sum):
+    u = lax.axis_index("zero") // 4
+    first, second = lengths[0, 0], lengths[0, 0] + lengths[0, 1]
     scale = HD**-0.5
     contract = (((1,), (1,)), ((), ()))
     dk_sum[...] = jnp.zeros_like(dk_sum)
     dv_sum[...] = jnp.zeros_like(dv_sum)
     kt[...] = kv[:, :HD].astype(F32).T.astype(BF)
+    vt[...] = kv[:, HD:].astype(F32).T.astype(BF)
 
     def work(block, keys):
         at = slice(block * ROWS, (block + 1) * ROWS)
         key_at = lax.broadcasted_iota(jnp.int32, (keys, ROWS), 0)
         query_at = keys - ROWS + lax.broadcasted_iota(jnp.int32, (1, ROWS), 1)
-        begin = jnp.where(query_at >= second, second, jnp.where(query_at >= first, first, 0))
-        allowed = (key_at <= query_at) & (key_at >= begin)
+        allowed = (key_at <= query_at) & (key_at >= begin_of(query_at, first, second))
         bias[:keys] = jnp.where(allowed, 0.0, NEGATIVE)
 
-        def one_head(head, carry):
-            query, grad = q[at, lanes(head, HD)], go[at, lanes(head, HD)]
+        def some_heads(step, carry):
+            def stack(ref):
+                parts = [ref[at, lanes(step * HEADS + i, HD)] for i in range(HEADS)]
+                return jnp.concatenate(parts, axis=0)
+
+            query, grad = stack(q), stack(go)
             key, value = kv[:keys, :HD], kv[:keys, HD:]
-            s = lax.dot_general(key, query, contract, preferred_element_type=F32) + bias[:keys]
+            s = lax.dot_general(key, query, contract, preferred_element_type=F32)
+            s = s + jnp.concatenate([bias[:keys]] * HEADS, axis=1)
             top = jnp.max(s, axis=0, keepdims=True)
             e = jnp.exp2((s - top) * (scale * LOG2E))
-            weights = e * (1.0 / jnp.sum(e, axis=0, keepdims=True))
-            low = weights.astype(BF)
+            share = 1.0 / jnp.sum(e, axis=0, keepdims=True)
+            low = (e * share).astype(BF)
+            attended = jnp.dot(vt[:, :keys], low, preferred_element_type=F32)
+            delta = jnp.sum(attended * grad.astype(F32).T, axis=0, keepdims=True)
             dw = lax.dot_general(value, grad, contract, preferred_element_type=F32)
-            delta = jnp.sum(low.astype(F32) * dw, axis=0, keepdims=True)
-            ds = (weights * (dw - delta)).astype(BF)
+            ds = (e * share * (dw - delta)).astype(BF)
             dv_sum[:keys] += jnp.dot(low, grad, preferred_element_type=F32)
             dk_sum[:keys] += jnp.dot(ds, query, preferred_element_type=F32)
             turned = jnp.dot(kt[:, :keys], ds, preferred_element_type=F32)
-            dq[at, lanes(head, HD)] = (turned.T * scale).astype(BF)
+            for i in range(HEADS):
+                part = turned[:, i * ROWS : (i + 1) * ROWS].T * scale
+                dq[at, lanes(step * HEADS + i, HD)] = part.astype(BF)
             return carry
 
-        lax.fori_loop(0, 8, one_head, 0)
-
+        lax.fori_loop(0, 8 // HEADS, some_heads, 0, unroll=1)
+
+    blocks = 512 // ROWS
     for half in range(2):
-        for block in range(2):
-            pl.when(u == half)(functools.partial(work, block, (half * 2 + block + 1) * ROWS))
+        for block in range(blocks):
+            keys = (half * blocks + block + 1) * ROWS
+            pl.when(u == half)(functools.partial(work, block, keys))
     dkv[:, :HD] = (dk_sum[...] * scale).astype(BF)
     dkv[:, HD:] = dv_sum[...].astype(BF)
 
 
-def attend(scalars, q_h, go_h, kv_h):
+def attend(lengths, q_h, go_h, kv_h):
     shape = jax.ShapeDtypeStruct
     return pl.pallas_call(
         attend_kernel,
@@ -357,12 +374,13 @@
         scratch_shapes=[
             pltpu.VMEM((1024, ROWS), F32),
             pltpu.VMEM((HD, 1024), BF),
+            pltpu.VMEM((HD, 1024), BF),
             pltpu.VMEM((1024, HD), F32),
             pltpu.VMEM((1024, HD), F32),
         ],
         out_shape=[shape((512, 1024), BF), shape((1024, 256), BF)],
         compiler_params=pltpu.CompilerParams(vmem_limit_bytes=56 << 20),
-    )(scalars, q_h, go_h, kv_h)
+    )(lengths, q_h, go_h, kv_h)
 
 
 def backward_kernel(
@@ -580,19 +598,55 @@
     )(dkv, dq_h, hid_g, wk, wv, cosine, sine)
 
 
+PARTS = 4
+
+
+def hand_on_kernel(*refs):
+    count = (len(refs) - 2) // 3
+    ins, outs, kept = refs[:count], refs[count : 2 * count], refs[2 * count : 3 * count]
+    come, go = refs[-2:]
+    loads, stores = [], []
+    for i in range(count):
+        size = ins[i].shape[0] // PARTS
+        for j in range(PARTS):
+            rows, at = pl.ds(j * size, size), i * PARTS + j
+            loads.append(pltpu.make_async_copy(ins[i].at[rows], kept[i].at[rows], come.at[at]))
+            stores.append(pltpu.make_async_copy(kept[i].at[rows], outs[i].at[rows], go.at[at]))
+    for one in loads:
+        one.start()
+    for load, store in zip(loads, stores):
+        load.wait()
+        store.start()
+    for one in stores:
+        one.wait()
+
+
+def hand_on(*arrays):
+    count = len(arrays)
+    return pl.pallas_call(
+        hand_on_kernel,
+        out_shape=[jax.ShapeDtypeStruct(one.shape, one.dtype) for one in arrays],
+        in_specs=[ANY] * count,
+        out_specs=[ANY] * count,
+        scratch_shapes=[
+            *[pltpu.VMEM(one.shape, one.dtype) for one in arrays],
+            pltpu.SemaphoreType.DMA((count * PARTS,)),
+            pltpu.SemaphoreType.DMA((count * PARTS,)),
+        ],
+    )(*arrays)
+
+
 def local(hidden, queries, grad_out, key_weight, value_weight, doc_lengths):
-    lengths = doc_lengths[0]
-    zero = lax.axis_index("zero")
-    cosine, sine = own_tables(lengths, zero * TOK)
-    hid_g, wk, wv, q_h, go_h, kv_h = forward(
-        hidden[0], queries[0], grad_out[0], key_weight, value_weight, cosine, sine
+    hid_g, wk, wv, q_h, go_h, kv_h, cosine, sine = forward(
+        hidden[0], queries[0], grad_out[0], key_weight, value_weight, doc_lengths
     )
-    scalars = jnp.concatenate([(zero // 4).astype(jnp.int32)[None], lengths])
     dq_h, dkv = attend(
-        scalars, q_h.reshape(512, 1024), go_h.reshape(512, 1024), kv_h.reshape(1024, 256)
+        doc_lengths, q_h.reshape(512, 1024), go_h.reshape(512, 1024), kv_h.reshape(1024, 256)
     )
-    dquery, dhidden, grad_key, grad_value = backward(
-        dkv.reshape(2, 4, TOK, 256), dq_h.reshape(4, TOK, 1024), hid_g, wk, wv, cosine, sine
+    dquery, dhidden, grad_key, grad_value = hand_on(
+        *backward(
+            dkv.reshape(2, 4, TOK, 256), dq_h.reshape(4, TOK, 1024), hid_g, wk, wv, cosine, sine
+        )
     )
     return dquery[None], dhidden[None], grad_key, grad_value
 

time: 149 us -> 136 us (0.913)
  local copies, waits for them, and re-layouts: 6.39 us -> 0 us
  other arithmetic: 2.98 us -> 0 us
  Pallas kernels: 137 us -> 135 us
    pallas_call x1, Pallas kernels: 14.7 us -> 8.72 us  [attend(): pl.pallas_call(attend_kernel, in_specs=[pl.BlockSpec(memory_space=pltpu.S...]
    unnamed x10 -> x0, local copies, waits for them, and re-layouts: 5.08 us -> none
    pallas_call x0 -> x1, Pallas kernels: none -> 3.02 us  [hand_on(): pl.pallas_call(hand_on_kernel, out_shape=[jax.ShapeDtypeStruct(one.shape,...]
where the time goes in v4:
time: 136 us
  Pallas kernels  135 us (99%)
    pallas_call x1, Pallas kernels, backward(): comm_call(backward_kernel, 1, (shape((TOK, 4096), BF), shape((TOK, WIDE),...  64.2 us
    pallas_call x1, Pallas kernels, forward(): comm_call(forward_kernel, 0, (shape((4, TOK, 2048), BF), shape(weights, B...  59 us
    pallas_call x1, Pallas kernels, attend(): pl.pallas_call(attend_kernel, in_specs=[pl.BlockSpec(memory_space=pltpu.S...  8.72 us
    pallas_call x1, Pallas kernels, hand_on(): pl.pallas_call(hand_on_kernel, out_shape=[jax.ShapeDtypeStruct(one.shape,...  3.02 us

profile of v4, /device:TPU:6, one launch (start us, length us, event | category | flops | bytes accessed | tf_op | source)
XLA Modules:
  0.0 135.8 jit_solution(16038947522759011772)
XLA Ops:
  0.6 59.0 %shard_map.102 = (bf16[4,128,2048]{2,1,0:T(8,128)(2,1)}, bf16[2,4,2,2,64,512]{5,4,3,2,1,0:T(8,128)(2,1)}, bf16[2,4,2,2,64,512]{5,4,3,2,1,0:T(8,128)(2,1)}, bf16[...) custom-call(bf16[128,8192]{1,0:T(8,128)(2,1)} %bitcast.10, ...), custom_call_target="tpu_custom_call" | custom-call | tf_op jit(solution)/shard_map/pallas_call | solution.py:279
  59.7 8.7 %shard_map.103 = (bf16[512,1024]{1,0:T(8,128)(2,1)}, bf16[1024,256]{1,0:T(8,128)(2,1)}) custom-call(s32[1,3]{1,0:T(1,128)} %lengths.3, bf16[512,1024]{1,0:T(8,128)(2,1)} %bitcast.14, bf16[512,1024]{1,0:T(8,128)(2,1)} %bitcast.15, bf16[1024,256]{1,0:T(8,128)(2,1)} %bitcast.16), custom_call_target="tpu_custom_call" | custom-call | tf_op jit(solution)/shard_map/pallas_call | solution.py:370
  68.4 64.2 %shard_map.104 = (bf16[128,4096]{1,0:T(8,128)(2,1)}, bf16[128,8192]{1,0:T(8,128)(2,1)}, f32[64,512]{1,0:T(8,128)}, f32[64,512]{1,0:T(8,128)}) custom-call(bf16[2,4,128,256]{3,2,1,0:T(8,128)(2,1)} %bitcast.17, bf16[4,128,1024]{2,1,0:T(8,128)(2,1)} %bitcast.13, bf16[4,128,2048]{2,1,0:T(8,128)(2,1)} %get-tuple-element.27.hid_in, ...), custom_call_target="tpu_custom_call" | custom-call | tf_op jit(solution)/shard_map/pallas_call | solution.py:569
  132.6 3.0 %shard_map.105 = (bf16[128,4096]{1,0:T(8,128)(2,1)}, bf16[128,8192]{1,0:T(8,128)(2,1)}, f32[64,512]{1,0:T(8,128)}, f32[64,512]{1,0:T(8,128)}) custom-call(bf16[128,4096]{1,0:T(8,128)(2,1)} %get-tuple-element.32.refs_0_, bf16[128,8192]{1,0:T(8,128)(2,1)} %get-tuple-element.33.refs_1_, f32[64,512]{1,0:T(8,128)} %get-tuple-element.34.refs_2_, ...), custom_call_target="tpu_custom_call" | custom-call | tf_op jit(solution)/shard_map/pallas_call | solution.py:626

commit v5 on v4

v5 whole, which is shorter than its diff:
```python
import functools

import jax
import jax.numpy as jnp
import numpy as np
from jax import lax
from jax.experimental import pallas as pl
from jax.experimental.pallas import tpu as pltpu
from jax.sharding import PartitionSpec as P

KV_HEADS = 4
HD = 128
ROPE_BASE = 500000.0
NEGATIVE = -1e30
LOG2E = 1.4426950408889634
MESH = pl.DeviceIdType.MESH
TOK = 128
WIDE = 8192
ANY = pl.BlockSpec(memory_space=pl.ANY)
VMEM = pl.BlockSpec(memory_space=pltpu.VMEM)
BF = jnp.bfloat16
F32 = jnp.float32


FREQUENCY = (ROPE_BASE ** (-2.0 * (np.arange(HD) % (HD // 2)) / HD)).astype(np.float32)


def begin_of(at, first, second):
    return jnp.where(at >= second, second, jnp.where(at >= first, first, 0))


def place():
    j, i = lax.axis_index("zero"), lax.axis_index("dp")
    return j // 4, j % 4, i // 4, (i // 2) % 2, i % 2


def device(u, x, z, w, c):
    return (u * 4 + x, z * 4 + w * 2 + c)


class Peers:
    def __init__(self):
        self.u, self.x, self.z, self.w, self.c = place()

    def along_x(self, d):
        return device(self.u, (self.x + d) % 4, self.z, self.w, self.c)

    def along_z(self, d):
        return device(self.u, self.x, (self.z + d) % 4, self.w, self.c)

    def y_at(self, d):
        y = (2 * self.u + self.w + d) % 4
        return y // 2, y % 2

    def along_y(self, d):
        u, w = self.y_at(d)
        return device(u, self.x, self.z, w, self.c)

    def in_group(self, du, dx):
        return device((self.u + du) % 2, (self.x + dx) % 4, self.z, self.w, self.c)

    def on_plane(self, dy, dx):
        u, w = self.y_at(dy)
        return device(u, (self.x + dx) % 4, self.z, w, self.c)

    def sibling(self):
        return device(self.u, self.x, self.z, self.w, 1 - self.c)


def meet(devices):
    barrier = pltpu.get_barrier_semaphore()
    for one in devices:
        pl.semaphore_signal(barrier, inc=1, device_id=one, device_id_type=MESH)
    pl.semaphore_wait(barrier, len(devices))


class Copies:
    def __init__(self, send, recv):
        self.send, self.recv, self.used = send, recv, 0

    def make(self, src, dst, to):
        at = self.used
        self.used += 1
        return pltpu.make_async_remote_copy(
            src_ref=src,
            dst_ref=dst,
            send_sem=self.send.at[at],
            recv_sem=self.recv.at[at],
            device_id=to,
            device_id_type=MESH,
        )

    def start(self, src, dst, to):
        copy = self.make(src, dst, to)
        copy.start()
        return copy


GROUP = [(du, dx) for du in (1, 0) for dx in (2, 1, 3, 0)][:-1]
PLANE = [(dy, dx) for dy in (2, 1, 3, 0) for dx in (2, 1, 3, 0)][:-1]
STEPS = (1, 3, 2)


def comm_call(kernel, number, outs, in_specs, out_specs, remote, local, scratch=()):
    return pl.pallas_call(
        kernel,
        out_shape=outs,
        in_specs=in_specs,
        out_specs=out_specs,
        scratch_shapes=[
            pltpu.SemaphoreType.DMA((remote,)),
            pltpu.SemaphoreType.DMA((remote,)),
            pltpu.SemaphoreType.DMA((local,)),
            *scratch,
        ],
        compiler_params=pltpu.CompilerParams(
            collective_id=number, has_side_effects=True, vmem_limit_bytes=63 << 20
        ),
    )


def lanes(at, size):
    return pl.ds(pl.multiple_of(at * size, size), size)


def turn(rows):
    return pltpu.roll(rows, HD // 2, 1)


WEIGHTS = (2, 4, 2, 2, 64, 512)
CONTRACT = (((1,), (1,)), ((), ()))


def whole_kernel(
    hidden, query, grad, wkey, wvalue, frequency, lengths,
    dq, dhidden, grad_key, grad_value,
    send, recv, here,
    hid, wk, wv, k_part, v_part, k_in, v_in, k_own, v_own, k_rows, v_rows,
    q_h, go_h, k_h, v_h, kt, vt, bias, ex, share, dk_sum, dv_sum, dk_out, dv_out, dq_h,
    k_came, v_came, rows_k, rows_v, turned, dh, low, away, other,
    key_in, value_in, key_sum, value_sum, key_last, value_last,
):
    p = Peers()
    u, x, z, w, c = p.u, p.x, p.z, p.w, p.c
    cp = Copies(send, recv)
    used = [0]
    scale = HD**-0.5
    first_end, second_end = lengths[0, 0], lengths[0, 0] + lengths[0, 1]

    def move(src, dst):
        copy = pltpu.make_async_copy(src, dst, here.at[used[0]])
        used[0] += 1
        copy.start()
        return copy

    own_key = move(wkey, wk.at[u, x, w, c])
    own_value = move(wvalue, wv.at[u, x, w, c])
    own_hidden = [
        move(hidden.at[:, lanes(piece * 4 + z, 256)], hid.at[z, :, pl.ds(piece * 256, 256)])
        for piece in range(8)
    ]
    own_heads = [
        move(query.at[:, lanes(x, 1024)], q_h.at[x]),
        move(grad.at[:, lanes(x, 1024)], go_h.at[x]),
    ]
    meet(
        [p.along_z(d) for d in STEPS]
        + [p.on_plane(dy, dx) for dy, dx in PLANE]
        + [p.sibling()]
    )
    key_y = [cp.start(wkey, wk.at[u, x, w, c], p.along_y(d)) for d in STEPS]
    value_x = [cp.start(wvalue, wv.at[u, x, w, c], p.along_x(d)) for d in STEPS]
    whole = []
    for d in STEPS:
        there, at = (z + d) % 4, cp.used
        for piece in range(8):
            cp.used = at
            cp.start(
                hidden.at[:, lanes(piece * 4 + there, 256)],
                hid.at[z, :, pl.ds(piece * 256, 256)],
                p.along_z(d),
            )
        cp.used = at
        came = (z + 4 - d) % 4
        whole.append(cp.make(hid.at[came], hid.at[came], p.along_z(d)))
    at = (u * 4 + x) * TOK + lax.broadcasted_iota(jnp.int32, (TOK, HD), 0)
    angles = (at - begin_of(at, first_end, second_end)).astype(F32) * frequency[...]
    sign = jnp.where(lax.broadcasted_iota(jnp.int32, (TOK, HD), 1) < HD // 2, -1.0, 1.0)
    cos, sin = jnp.cos(angles), sign * jnp.sin(angles)
    dk_sum[...] = jnp.zeros_like(dk_sum)
    dv_sum[...] = jnp.zeros_like(dv_sum)

    @pl.when(u == 0)
    def _():
        k_h[1] = jnp.zeros((4, TOK, HD), BF)
        v_h[1] = jnp.zeros((4, TOK, HD), BF)

    @pl.when(u == 1)
    def _():
        k_came[0] = jnp.zeros((4, TOK, HD), BF)
        v_came[0] = jnp.zeros((4, TOK, HD), BF)

    own_key.wait()
    for one in key_y:
        one.wait_recv()
    column = wk.at[:, x, :, c]
    key_x = [cp.start(column, column, p.along_x(d)) for d in STEPS]
    to_core = [cp.start(column, column, p.sibling())]
    own_value.wait()
    for one in value_x:
        one.wait_recv()
    row = wv.at[u, :, w, c]
    value_y = [cp.start(row, row, p.along_y(d)) for d in STEPS]
    to_core.append(cp.start(row, row, p.sibling()))
    sent_heads = []
    for source, target in ((query, q_h), (grad, go_h)):
        for d in STEPS:
            sent_heads.append(
                cp.start(source.at[:, lanes((x + d) % 4, 1024)], target.at[x], p.along_x(d))
            )
    for d, one in zip(STEPS, key_x):
        one.wait_recv()
        column = wk.at[:, (x + 4 - d) % 4, :, c]
        to_core.append(cp.start(column, column, p.sibling()))
    for d, one in zip(STEPS, value_y):
        one.wait_recv()
        from_u, from_w = p.y_at(4 - d)
        row = wv.at[from_u, :, from_w, c]
        to_core.append(cp.start(row, row, p.sibling()))
    for one in own_hidden:
        one.wait()
    for one in to_core:
        one.wait_recv()

    def project(slot, weights):
        return jnp.dot(hid[slot], weights[...].reshape(2048, 512), preferred_element_type=F32)

    k_own[...] = project(z, wk)
    k_back, v_back = [], []
    for number, d in enumerate(STEPS):
        whole[number].wait_recv()
        k_part[number] = project((z + 4 - d) % 4, wk)
        k_back.append(cp.start(k_part.at[number], k_in.at[number], p.along_z(4 - d)))
    for number, d in enumerate(STEPS):
        v_part[number] = project((z + 4 - d) % 4, wv).astype(BF)
        v_back.append(cp.start(v_part.at[number], v_in.at[number], p.along_z(4 - d)))
    v_own[...] = project(z, wv)

    def transpose(k, carry):
        block = hid[:, :, lanes(k, 128)].reshape(512, 128)
        turned[k] = block.astype(F32).T.astype(BF)
        return carry

    lax.fori_loop(0, 16, transpose, 0)

    def exchange(source, target, low_to_high):
        across = [cp.make(source(dx, 1), target.at[u, x], p.in_group(1, dx)) for dx in (2, 1, 3, 0)]

        @pl.when(u == (0 if low_to_high else 1))
        def _():
            for one in across:
                one.start()

        own = move(source(0, 0), target.at[u, x])
        near = [cp.start(source(dx, 0), target.at[u, x], p.along_x(dx)) for dx in STEPS]

        def receive():
            own.wait()
            for one in near:
                one.wait_recv()

            @pl.when(u == (1 if low_to_high else 0))
            def _():
                for one in across:
                    one.wait_recv()

        def sent():
            for one in near:
                one.wait_send()

            @pl.when(u == (0 if low_to_high else 1))
            def _():
                for one in across:
                    one.wait_send()

        return receive, sent

    def head_of(rows):
        return lambda dx, du: rows.at[:, lanes((x + dx) % 4, HD)]

    def owner_of(rows):
        return lambda dx, du: rows.at[0 if du else u, (x + dx) % 4]

    for one in k_back:
        one.wait_recv()
    for h in range(KV_HEADS):
        part = slice(h * HD, (h + 1) * HD)
        k = k_own[:, part]
        for number in range(3):
            k = k + k_in[number, :, part]
        k_rows[:, part] = (k * cos + turn(k) * sin).astype(BF)
    receive_k, sent_k = exchange(head_of(k_rows), k_h, True)
    for one in own_heads:
        one.wait()
    for one in sent_heads:
        one.wait_recv()
    receive_k()
    kt[...] = k_h[...].reshape(1024, HD).astype(F32).T.astype(BF)

    def stack(ref, block):
        parts = [ref[block, :, h * HD : (h + 1) * HD] for h in range(8)]
        return jnp.concatenate(parts, axis=0)

    def either(work, block):
        for half in range(2):
            pl.when(u == half)(functools.partial(work, block, (half * 4 + block + 1) * TOK))

    def weigh(block, keys):
        key_at = lax.broadcasted_iota(jnp.int32, (keys, TOK), 0)
        query_at = keys - TOK + lax.broadcasted_iota(jnp.int32, (1, TOK), 1)
        allowed = (key_at <= query_at) & (key_at >= begin_of(query_at, first_end, second_end))
        bias[:keys] = jnp.where(allowed, 0.0, NEGATIVE)
        key = k_h[...].reshape(1024, HD)[:keys]
        s = lax.dot_general(key, stack(q_h, block), CONTRACT, preferred_element_type=F32)
        s = s + jnp.concatenate([bias[:keys]] * 8, axis=1)
        top = jnp.max(s, axis=0, keepdims=True)
        e = jnp.exp2((s - top) * (scale * LOG2E))
        ex[block, :keys] = e
        inverse = 1.0 / jnp.sum(e, axis=0, keepdims=True)
        share[block, 0:1] = inverse
        weights = (e * inverse).astype(BF)
        dv_sum[:keys] += jnp.dot(weights, stack(go_h, block), preferred_element_type=F32)

    def differentiate(block, keys):
        grads = stack(go_h, block)
        value = v_h[...].reshape(1024, HD)[:keys]
        inverse = share[block, 0:1]
        weights = ex[block, :keys] * inverse
        attended = jnp.dot(vt[:, :keys], weights.astype(BF), preferred_element_type=F32)
        delta = jnp.sum(attended * grads.astype(F32).T, axis=0, keepdims=True)
        dw = lax.dot_general(value, grads, CONTRACT, preferred_element_type=F32)
        ds = (weights * (dw - delta)).astype(BF)
        dk_sum[:keys] += jnp.dot(ds, stack(q_h, block), preferred_element_type=F32)
        back = jnp.dot(kt[:, :keys], ds, preferred_element_type=F32)
        for h in range(8):
            part = back[:, h * TOK : (h + 1) * TOK].T * scale
            dq_h[block, :, h * HD : (h + 1) * HD] = part.astype(BF)

    either(weigh, 0)
    either(weigh, 1)
    for one in v_back:
        one.wait_recv()
    v = v_own[...]
    for number in range(3):
        v = v + v_in[number].astype(F32)
    v_rows[...] = v.astype(BF)
    receive_v, sent_v = exchange(head_of(v_rows), v_h, True)
    either(weigh, 2)
    either(weigh, 3)
    dv_out[...] = dv_sum[...].astype(BF).reshape(2, 4, TOK, HD)
    receive_dv, sent_dv = exchange(owner_of(dv_out), v_came, False)
    receive_v()
    vt[...] = v_h[...].reshape(1024, HD).astype(F32).T.astype(BF)
    either(differentiate, 0)
    either(differentiate, 1)
    receive_dv()
    for h in range(KV_HEADS):
        total = v_came[0, h].astype(F32) + v_came[1, h].astype(F32)
        rows_v[z, :, h * HD : (h + 1) * HD] = total.astype(BF)
    sent_z = [cp.start(rows_v.at[z], rows_v.at[z], p.along_z(d)) for d in STEPS]
    either(differentiate, 2)
    either(differentiate, 3)
    dk_out[...] = (dk_sum[...] * scale).astype(BF).reshape(2, 4, TOK, HD)
    receive_dk, sent_dk = exchange(owner_of(dk_out), k_came, False)
    later = [move(dq_h.at[x], dq.at[:, lanes(x, 1024)])]
    receive_dk()
    for h in range(KV_HEADS):
        dk = k_came[0, h].astype(F32) + k_came[1, h].astype(F32)
        rows_k[z, :, h * HD : (h + 1) * HD] = (dk * cos - turn(dk) * sin).astype(BF)
    sent_zk = [cp.start(rows_k.at[z], rows_k.at[z], p.along_z(d)) for d in STEPS]
    sent = [
        cp.start(dq_h.at[(x + d) % 4], dq.at[:, lanes(x, 1024)], p.along_x(d)) for d in STEPS
    ]

    def hidden_rows(slot, number):
        def one(piece, carry):
            key = wk[piece // 4, piece % 4].reshape(256, 512)
            value = wv[piece // 4, piece % 4].reshape(256, 512)
            total = lax.dot_general(
                rows_k[slot], key, CONTRACT, preferred_element_type=F32
            ) + lax.dot_general(rows_v[slot], value, CONTRACT, preferred_element_type=F32)
            dh[number, :, lanes(piece, 256)] = total.astype(BF)
            return carry

        lax.fori_loop(0, 8, one, 0)

    hidden_rows(z, 3)
    for piece in range(8):
        later.append(
            move(dh.at[3, :, pl.ds(piece * 256, 256)], dhidden.at[:, lanes(piece * 4 + z, 256)])
        )
    returned = []
    for number, d in enumerate(STEPS):
        sent_z[number].wait_recv()
        sent_zk[number].wait_recv()
        hidden_rows((z + 4 - d) % 4, number)
        at = cp.used
        for piece in range(8):
            cp.used = at
            cp.start(
                dh.at[number, :, pl.ds(piece * 256, 256)],
                dhidden.at[:, lanes(piece * 4 + z, 256)],
                p.along_z(4 - d),
            )
        cp.used = at
        returned.append(cp.make(dh.at[number], dh.at[number], p.along_z(4 - d)))
    order = PLANE + [(0, 0)]
    swapped, key_out, value_out = [], {}, {}

    def mine(k):
        return ex.at[0, pl.ds(k * 64, 64)]

    def pass_on(k):
        swapped[k].wait_recv()
        low[k] = (mine(k)[...] + other[k].astype(F32)).astype(BF)
        dy, dx = order[k]
        if dx:
            key_out[dy, dx] = cp.start(
                low.at[k, :, pl.ds(0, 512)],
                key_in.at[dx - 1, (2 * u + w + dy) % 4],
                p.along_x(dx),
            )
        if dy:
            value_out[dy, dx] = cp.start(
                low.at[k, :, pl.ds(512, 512)], value_in.at[dy - 1, (x + dx) % 4], p.along_y(dy)
            )

    for k, (dy, dx) in enumerate(order):
        tu, tw = p.y_at(dy)
        block = (tu * 4 + (x + dx) % 4) * 2 + tw
        for lane, rows in ((0, rows_k), (512, rows_v)):
            product = jnp.dot(
                turned[block], rows[...].reshape(512, 512), preferred_element_type=F32
            )
            kept = jnp.where(c == 0, product[:64], product[64:])
            given = jnp.where(c == 0, product[64:], product[:64])
            mine(k)[:, lane : lane + 512] = kept
            away[k, :, lane : lane + 512] = given.astype(BF)
        swapped.append(cp.start(away.at[k], other.at[k], p.sibling()))
        if k >= 2:
            pass_on(k - 2)
    pass_on(14)
    pass_on(15)
    last = []
    for d in (2, 1, 3, 0):
        for one in range(1, 4):
            key_out[d, one].wait_recv()
        total = low[order.index((d, 0)), :, :512].astype(F32)
        for one in range(3):
            total = total + key_in[one, (2 * u + w + d) % 4].astype(F32)
        if d:
            key_sum[d - 1] = total.astype(BF)
            last.append(cp.start(key_sum.at[d - 1], key_last.at[d - 1], p.along_y(d)))
        else:
            grad_key[...] = total
        for one in range(1, 4):
            value_out[one, d].wait_recv()
        total = low[order.index((0, d)), :, 512:].astype(F32)
        for one in range(3):
            total = total + value_in[one, (x + d) % 4].astype(F32)
        if d:
            value_sum[d - 1] = total.astype(BF)
            last.append(cp.start(value_sum.at[d - 1], value_last.at[d - 1], p.along_x(d)))
        else:
            grad_value[...] = total
    for one in last:
        one.wait_recv()
    for one in range(3):
        grad_key[...] += key_last[one].astype(F32)
        grad_value[...] += value_last[one].astype(F32)
    for one in returned + sent:
        one.wait_recv()
    for one in (sent_k, sent_v, sent_dv, sent_dk):
        one()
    for group in (
        key_y, value_x, whole, key_x, value_y, to_core, sent_heads, k_back, v_back,
        sent_z, sent_zk, sent, returned, swapped, key_out.values(), value_out.values(), last,
    ):
        for one in group:
            one.wait_send()
    for one in later:
        one.wait()


def whole_layer(hidden, query, grad, wkey, wvalue, lengths):
    shape, vmem = jax.ShapeDtypeStruct, pltpu.VMEM
    return comm_call(
        whole_kernel,
        0,
        (
            shape((TOK, 4096), BF),
            shape((TOK, WIDE), BF),
            shape((64, 512), F32),
            shape((64, 512), F32),
        ),
        [ANY] * 5 + [VMEM, pl.BlockSpec(memory_space=pltpu.SMEM)],
        (ANY, ANY, VMEM, VMEM),
        124,
        28,
        (
            vmem((4, TOK, 2048), BF),
            vmem(WEIGHTS, BF),
            vmem(WEIGHTS, BF),
            vmem((3, TOK, 512), F32),
            vmem((3, TOK, 512), BF),
            vmem((3, TOK, 512), F32),
            vmem((3, TOK, 512), BF),
            vmem((TOK, 512), F32),
            vmem((TOK, 512), F32),
            vmem((TOK, 512), BF),
            vmem((TOK, 512), BF),
            vmem((4, TOK, 1024), BF),
            vmem((4, TOK, 1024), BF),
            vmem((2, 4, TOK, HD), BF),
            vmem((2, 4, TOK, HD), BF),
            vmem((HD, 1024), BF),
            vmem((HD, 1024), BF),
            vmem((1024, TOK), F32),
            vmem((4, 1024, 1024), F32),
            vmem((4, 8, 1024), F32),
            vmem((1024, HD), F32),
            vmem((1024, HD), F32),
            vmem((2, 4, TOK, HD), BF),
            vmem((2, 4, TOK, HD), BF),
            vmem((4, TOK, 1024), BF),
            vmem((2, 4, TOK, HD), BF),
            vmem((2, 4, TOK, HD), BF),
            vmem((4, TOK, 512), BF),
            vmem((4, TOK, 512), BF),
            vmem((16, TOK, 512), BF),
            vmem((4, TOK, 2048), BF),
            vmem((16, 64, 1024), BF),
            vmem((16, 64, 1024), BF),
            vmem((16, 64, 1024), BF),
            vmem((3, 4, 64, 512), BF),
            vmem((3, 4, 64, 512), BF),
            *[vmem((3, 64, 512), BF)] * 4,
        ),
    )(hidden, query, grad, wkey, wvalue, jnp.asarray(FREQUENCY)[None], lengths)


PARTS = 4


def hand_on_kernel(*refs):
    count = (len(refs) - 2) // 3
    ins, outs, kept = refs[:count], refs[count : 2 * count], refs[2 * count : 3 * count]
    come, go = refs[-2:]
    loads, stores = [], []
    for i in range(count):
        size = ins[i].shape[0] // PARTS
        for j in range(PARTS):
            rows, at = pl.ds(j * size, size), i * PARTS + j
            loads.append(pltpu.make_async_copy(ins[i].at[rows], kept[i].at[rows], come.at[at]))
            stores.append(pltpu.make_async_copy(kept[i].at[rows], outs[i].at[rows], go.at[at]))
    for one in loads:
        one.start()
    for load, store in zip(loads, stores):
        load.wait()
        store.start()
    for one in stores:
        one.wait()


def hand_on(*arrays):
    count = len(arrays)
    return pl.pallas_call(
        hand_on_kernel,
        out_shape=[jax.ShapeDtypeStruct(one.shape, one.dtype) for one in arrays],
        in_specs=[ANY] * count,
        out_specs=[ANY] * count,
        scratch_shapes=[
            *[pltpu.VMEM(one.shape, one.dtype) for one in arrays],
            pltpu.SemaphoreType.DMA((count * PARTS,)),
            pltpu.SemaphoreType.DMA((count * PARTS,)),
        ],
    )(*arrays)


def local(hidden, queries, grad_out, key_weight, value_weight, doc_lengths):
    dquery, dhidden, grad_key, grad_value = hand_on(
        *whole_layer(
            hidden[0], queries[0], grad_out[0], key_weight, value_weight, doc_lengths
        )
    )
    return dquery[None], dhidden[None], grad_key, grad_value


def solution(mesh):
    return jax.shard_map(
        local,
        mesh=mesh,
        in_specs=(
            P("dp", "zero", None),
            P("dp", "zero", None),
            P("dp", "zero", None),
            P(("zero", "dp"), None),
            P(("zero", "dp"), None),
            P("dp", None),
        ),
        out_specs=(
            P("dp", "zero", None),
            P("dp", "zero", None),
            P(("zero", "dp"), None),
            P(("zero", "dp"), None),
        ),
        check_vma=False,
    )
```

time: 136 us -> 113 us (0.83)
  Pallas kernels: 135 us -> 111 us
    pallas_call x3 -> x1, Pallas kernels: 132 us -> 108 us  [whole_layer(): comm_call(whole_kernel, 0, (shape((TOK, 4096), BF), shape((TOK, WIDE), BF...]
where the time goes in v5:
time: 113 us; the launch traced here: 112 us
  Pallas kernels  111 us (98%)
    pallas_call x1, Pallas kernels, whole_layer(): comm_call(whole_kernel, 0, (shape((TOK, 4096), BF), shape((TOK, WIDE), BF...  108 us
    pallas_call x1, Pallas kernels, hand_on(): pl.pallas_call(hand_on_kernel, out_shape=[jax.ShapeDtypeStruct(one.shape,...  3.02 us

profile of v5, /device:TPU:6, one launch (start us, length us, event | category | flops | bytes accessed | tf_op | source)
XLA Modules:
  0.0 111.9 jit_solution(6403668707165113730)
XLA Ops:
  0.6 108.0 %shard_map.102 = (bf16[128,4096]{1,0:T(8,128)(2,1)}, bf16[128,8192]{1,0:T(8,128)(2,1)}, f32[64,512]{1,0:T(8,128)}, f32[64,512]{1,0:T(8,128)}) custom-call(bf16[128,8192]{1,0:T(8,128)(2,1)} %bitcast.5, bf16[128,4096]{1,0:T(8,128)(2,1)} %bitcast.6, bf16[128,4096]{1,0:T(8,128)(2,1)} %bitcast.7, bf16[64,512]{1,0:T(8,128)(2,1)} %wkey.1, bf16[64,512]{1,0:T(8,128)(2,1)} %wvalue.1, ...), custom_call_target="tpu_custom_call" | custom-call | tf_op jit(solution)/shard_map/pallas_call | solution.py:497
  108.7 3.0 %shard_map.103 = (bf16[128,4096]{1,0:T(8,128)(2,1)}, bf16[128,8192]{1,0:T(8,128)(2,1)}, f32[64,512]{1,0:T(8,128)}, f32[64,512]{1,0:T(8,128)}) custom-call(bf16[128,4096]{1,0:T(8,128)(2,1)} %get-tuple-element.12.refs_0_, bf16[128,8192]{1,0:T(8,128)(2,1)} %get-tuple-element.13.refs_1_, f32[64,512]{1,0:T(8,128)} %get-tuple-element.14.refs_2_, ...), custom_call_target="tpu_custom_call" | custom-call | tf_op jit(solution)/shard_map/pallas_call | solution.py:577

commit v6 on v5

--- a/solution.py
+++ b/solution.py
@@ -153,6 +153,14 @@
         copy.start()
         return copy
 
+    barrier = pltpu.get_barrier_semaphore()
+    met = (
+        [p.along_z(d) for d in STEPS]
+        + [p.on_plane(dy, dx) for dy, dx in PLANE]
+        + [p.sibling()]
+    )
+    for one in met:
+        pl.semaphore_signal(barrier, inc=1, device_id=one, device_id_type=MESH)
     own_key = move(wkey, wk.at[u, x, w, c])
     own_value = move(wvalue, wv.at[u, x, w, c])
     own_hidden = [
@@ -163,11 +171,7 @@
         move(query.at[:, lanes(x, 1024)], q_h.at[x]),
         move(grad.at[:, lanes(x, 1024)], go_h.at[x]),
     ]
-    meet(
-        [p.along_z(d) for d in STEPS]
-        + [p.on_plane(dy, dx) for dy, dx in PLANE]
-        + [p.sibling()]
-    )
+    pl.semaphore_wait(barrier, len(met))
     key_y = [cp.start(wkey, wk.at[u, x, w, c], p.along_y(d)) for d in STEPS]
     value_x = [cp.start(wvalue, wv.at[u, x, w, c], p.along_x(d)) for d in STEPS]
     whole = []
@@ -243,7 +247,7 @@
         k_back.append(cp.start(k_part.at[number], k_in.at[number], p.along_z(4 - d)))
     for number, d in enumerate(STEPS):
         v_part[number] = project((z + 4 - d) % 4, wv).astype(BF)
-        v_back.append(cp.start(v_part.at[number], v_in.at[number], p.along_z(4 - d)))
+        v_back.append(cp.make(v_part.at[number], v_in.at[number], p.along_z(4 - d)))
     v_own[...] = project(z, wv)
 
     def transpose(k, carry):
@@ -300,6 +304,8 @@
             k = k + k_in[number, :, part]
         k_rows[:, part] = (k * cos + turn(k) * sin).astype(BF)
     receive_k, sent_k = exchange(head_of(k_rows), k_h, True)
+    for one in v_back:
+        one.start()
     for one in own_heads:
         one.wait()
     for one in sent_heads:

time: 113 us -> 114 us (level)
  no operation moved by 1% of the time
where the time goes in v6:
time: 114 us; the launch traced here: 112 us
  Pallas kernels  111 us (97%)
    pallas_call x1, Pallas kernels, whole_layer(): comm_call(whole_kernel, 0, (shape((TOK, 4096), BF), shape((TOK, WIDE), BF...  108 us
    pallas_call x1, Pallas kernels, hand_on(): pl.pallas_call(hand_on_kernel, out_shape=[jax.ShapeDtypeStruct(one.shape,...  3.02 us

profile of v6, /device:TPU:6, one launch (start us, length us, event | category | flops | bytes accessed | tf_op | source)
XLA Modules:
  0.0 112.3 jit_solution(1292691409500080163)
XLA Ops:
  0.6 108.5 %shard_map.102 = (bf16[128,4096]{1,0:T(8,128)(2,1)}, bf16[128,8192]{1,0:T(8,128)(2,1)}, f32[64,512]{1,0:T(8,128)}, f32[64,512]{1,0:T(8,128)}) custom-call(bf16[128,8192]{1,0:T(8,128)(2,1)} %bitcast.5, bf16[128,4096]{1,0:T(8,128)(2,1)} %bitcast.6, bf16[128,4096]{1,0:T(8,128)(2,1)} %bitcast.7, bf16[64,512]{1,0:T(8,128)(2,1)} %wkey.1, bf16[64,512]{1,0:T(8,128)(2,1)} %wvalue.1, ...), custom_call_target="tpu_custom_call" | custom-call | tf_op jit(solution)/shard_map/pallas_call | solution.py:503
  109.1 3.0 %shard_map.103 = (bf16[128,4096]{1,0:T(8,128)(2,1)}, bf16[128,8192]{1,0:T(8,128)(2,1)}, f32[64,512]{1,0:T(8,128)}, f32[64,512]{1,0:T(8,128)}) custom-call(bf16[128,4096]{1,0:T(8,128)(2,1)} %get-tuple-element.12.refs_0_, bf16[128,8192]{1,0:T(8,128)(2,1)} %get-tuple-element.13.refs_1_, f32[64,512]{1,0:T(8,128)} %get-tuple-element.14.refs_2_, ...), custom_call_target="tpu_custom_call" | custom-call | tf_op jit(solution)/shard_map/pallas_call | solution.py:583
